TPU v7x, 128 devices: a whole 4x4x4 slice. The times are simulated.
128 devices in a mesh: row: 16 (over z, x_hi, core), col: 8 (over y, x_lo).
Axes of the slice: x: 4 (x_hi: 2, x_lo: 2; x = x_hi * 2 + x_lo), y: 4, z: 4, core: 2. Of those that a mesh axis runs over, the one named last changes fastest.
Arguments:
- amplitudes: bfloat16 [512, 512, 256], P('row', 'col'), may hold values from -6 to 6
- integrals: bfloat16 [512, 512, 256], P('row', 'col'), may hold values from -0.0625 to 0.0625
- occ_energy: float32 [16], replicated, may hold values from -1.5 to -0.5
- vir_energy: float32 [512], replicated, may hold values from 0.5 to 3
Outputs:
- updated: float32 [512, 512, 256], P('row', 'col')
All inputs are finite; a program needn't handle non-finite values.
Results may differ from a plain program's by a relative error of at most 0.0017.
Values may be sent and summed in bfloat16 or wider, within the bound.
A program may use at most 192 MiB of HBM per device.

v0:
```python
import jax
import jax.numpy as jnp
from jax import lax
from jax.sharding import PartitionSpec as P

OCC = 16


def local(amplitudes, integrals, occ_energy, vir_energy):
    block_a, block_b, pair_count = amplitudes.shape
    amp_local = amplitudes.reshape(block_a, block_b, OCC, OCC)
    int_local = integrals.reshape(integrals.shape[0], integrals.shape[1], OCC, OCC)
    amp_rows = lax.all_gather(amp_local, "col", axis=1, tiled=True)
    cycle_term = jnp.einsum(
        "acik,cbkj->abij",
        amp_rows,
        lax.all_gather(int_local, "row", axis=0, tiled=True),
        preferred_element_type=jnp.float32,
    )
    antisym = cycle_term - cycle_term.transpose(0, 1, 3, 2)
    cross_flat = antisym.reshape(block_a, block_b, pair_count)
    spread = lax.all_to_all(
        cross_flat.astype(jnp.bfloat16), "col", split_axis=0, concat_axis=1, tiled=True
    ).astype(cross_flat.dtype)
    crossed = lax.all_to_all(
        spread.astype(jnp.bfloat16), ("row", "col"), split_axis=1, concat_axis=0, tiled=True
    ).astype(spread.dtype)
    turned = crossed.transpose(1, 0, 2)
    mirror = lax.all_to_all(
        turned.astype(jnp.bfloat16), "col", split_axis=1, concat_axis=0, tiled=True
    ).astype(turned.dtype)
    row_pos = lax.axis_index("row")
    col_pos = lax.axis_index("col")
    vir_rows = lax.dynamic_slice_in_dim(vir_energy, row_pos * block_a, block_a)
    vir_cols = lax.dynamic_slice_in_dim(vir_energy, col_pos * block_b, block_b)
    denominator = (
        occ_energy[None, None, :, None]
        + occ_energy[None, None, None, :]
        - vir_rows[:, None, None, None]
        - vir_cols[None, :, None, None]
    )
    denominator = denominator.reshape(block_a, block_b, pair_count)
    return amplitudes.astype(jnp.float32) + (cross_flat - mirror) / denominator


def solution(mesh):
    placed = (P("row", "col", None), P("row", "col", None), P(), P())
    return jax.shard_map(
        local, mesh=mesh, in_specs=placed, out_specs=P("row", "col", None), check_vma=False
    )
```

profile of v0, /device:TPU:11, one launch (start us, length us, event | category | flops | bytes accessed | tf_op | source)
XLA Modules:
  0.0 1036.8 jit_solution(10674862283106920592)
XLA Ops:
  6.5 0.0 copy-start.1
  6.5 0.0 all-gather.5.cloned.1.call-start
  6.5 4.8 copy.61
  11.3 0.0 all-gather.5.cloned.1.call-update
  11.3 0.0 all-gather.3.cloned.1.call-start
  11.4 0.0 copy-done.1
  11.4 1.8 copy.60
  13.2 0.0 all-gather.3.cloned.1.call-update
  13.2 640.8 %all-gather.5.cloned.1.call-done = bf16[32,512,16,16]{0,3,2,1:T(8,128)(2,1)} async-done(((bf16[32,64,16,16]{0,3,2,1:T(8,128)(2,1)}), bf16[32,512,16,16]{0,3,2,1:T(8,128)(2,1)}) %all-gather.5.cloned.1.call-update) | async-done | bytes 8388624 | tf_op jit(solution)/shard_map/all_gather | solution.py:13
  654.0 34.2 %copy.63 = bf16[32,512,16,16]{1,0,3,2:T(8,128)(2,1)} copy(bf16[32,512,16,16]{0,3,2,1:T(8,128)(2,1)} %all-gather.5.cloned.1.call-done) | data formatting | bytes 16777216 | tf_op jit(solution)/shard_map/all_gather | solution.py:13
  688.2 155.0 %all-gather.3.cloned.1.call-done = bf16[512,64,16,16]{1,3,2,0:T(8,128)(2,1)} async-done(((bf16[32,64,16,16]{1,3,2,0:T(8,128)(2,1)}), bf16[512,64,16,16]{1,3,2,0:T(8,128)(2,1)}) %all-gather.3.cloned.1.call-update) | async-done | bytes 16777232 | tf_op jit(solution)/shard_map/all_gather | solution.py:17
  843.2 42.8 %copy.73 = bf16[512,64,16,16,1]{0,3,2,4,1:T(8,128)(2,1)} copy(bf16[512,64,16,16,1]{1,3,2,0,4:T(8,128)(2,1)} %bitcast.38) | data formatting | bytes 33554432 | tf_op jit(solution)/shard_map/all_gather | solution.py:17
  886.0 41.2 %fusion = f32[64,16,32,16,1]{2,1,4,3,0:T(8,128)} fusion(bf16[512,64,16,16,1]{0,3,2,4,1:T(8,128)(2,1)} %copy.73, bf16[32,512,16,16]{1,0,3,2:T(8,128)(2,1)} %copy.63), kind=kOutput, calls=%fused_computation.1 | convolution fusion | flops 8589934592 | bytes 27262976 | tf_op jit(solution)/shard_map/acik,cbkj->abij/dot_general | solution.py:14
  927.2 13.4 %bitcast_subtract_fusion = f32[32,64,16,16]{0,2,3,1:T(8,128)} fusion(f32[64,16,32,16,1]{2,1,4,3,0:T(8,128)} %fusion, f32[64,16,32,16]{2,1,3,0:T(8,128)} %bitcast.37), kind=kLoop, calls=%fused_computation | loop fusion | flops 524288 | bytes 6291456 | tf_op jit(solution)/shard_map/sub | solution.py:20
  940.7 8.8 copy.65
  949.5 2.5 bitcast_convert_fusion
  952.0 0.8 copy.66
  952.9 19.1 %all_to_all.36 = bf16[32,64,256]{2,1,0:T(8,128)(2,1)S(1)} all-to-all(bf16[32,64,256]{2,1,0:T(8,128)(2,1)S(1)} %copy.66), channel_id=1, replica_groups=mesh['row'=16,'col'=8] {'col'}, dimensions={0} | all-to-all | bytes 2097152 | tf_op jit(solution)/shard_map/all_to_all | solution.py:22
  972.0 0.1 copy.67
  972.1 0.0 copy-start
  972.1 0.8 copy.68
  972.9 22.9 %all_to_all.37 = bf16[4,512,256]{2,0,1:T(4,128)(2,1)S(1)} all-to-all(bf16[4,512,256]{2,0,1:T(4,128)(2,1)S(1)} %copy.68), channel_id=1, replica_groups=mesh['row'=16,'col'=8] {'row','col'}, dimensions={1} | all-to-all | bytes 2097152 | tf_op jit(solution)/shard_map/all_to_all | solution.py:25
  995.8 0.0 copy-start.3
  995.8 0.0 copy-start.2
  995.8 1.4 copy.69
  997.2 5.8 all-to-all-start.2
  1003.0 0.0 copy-done
  1003.0 1.8 copy.59
  1004.8 0.0 copy-done.3
  1004.8 0.1 dynamic_slice.7
  1004.9 0.1 dynamic_slice.6
  1005.0 0.0 copy-done.2
  1005.0 0.1 broadcast_add_fusion
  1005.0 0.1 add.34
  1005.1 0.1 broadcast_subtract_fusion
  1005.2 11.9 %all-to-all-done.2 = bf16[4,512,256]{2,0,1:T(4,128)(2,1)S(1)} async-done(((bf16[4,512,256]{2,0,1:T(4,128)(2,1)}), bf16[4,512,256]{2,0,1:T(4,128)(2,1)S(1)}, u32[]{:S(2)}, u32[]{:S(2)}) %all-to-all-start.2) | async-done | bytes 1048608 | tf_op jit(solution)/shard_map/all_to_all | solution.py:29
  1017.1 0.1 copy.70
  1017.2 0.3 convert_bitcast_fusion
  1017.5 2.7 copy.71
  1020.2 5.9 fusion.3
  1026.1 3.8 copy.72
Async XLA Ops:
  6.5 4.9 copy-start.1
  6.5 647.4 %all-gather.5.cloned.1.call-start = ((), (), s32[]{:S(2)}) async-start(), calls=%async_computation.4 | async-start | bytes 37748736 | tf_op jit(solution)/shard_map/all_gather | solution.py:13
  11.3 831.9 %all-gather.3.cloned.1.call-start = ((), (), s32[]{:S(2)}) async-start(), calls=%async_computation.3 | async-start | bytes 35651584 | tf_op jit(solution)/shard_map/all_gather | solution.py:17
  972.1 31.0 %copy-start = (bf16[32,64,256]{2,1,0:T(8,128)(2,1)S(1)}, bf16[32,64,256]{2,1,0:T(8,128)(2,1)}, u32[]{:S(2)}) copy-start(bf16[32,64,256]{2,1,0:T(8,128)(2,1)} %param.4) | copy-start | bytes 3145732
  995.8 9.0 copy-start.3
  995.8 9.2 copy-start.2
  997.2 19.9 %all-to-all-start.2 = ((bf16[4,512,256]{2,0,1:T(4,128)(2,1)}), bf16[4,512,256]{2,0,1:T(4,128)(2,1)S(1)}, u32[]{:S(2)}, u32[]{:S(2)}) async-start(bf16[4,512,256]{2,0,1:T(4,128)(2,1)} %bitcast.15), calls=%async_computation.2 | async-start | bytes 2097152 | tf_op jit(solution)/shard_map/all_to_all | solution.py:29
Sparse Core Ops, SparseCore 0:
  11.5 642.4 all-gather.4
  656.4 186.7 all-gather.2
where the time goes:
time: 1040 us
  waiting for transfers between devices  808 us (78%)
  local copies, waits for them, and re-layouts  104 us (10%)
  blocking collectives  42 us (4%)
  matrix products  41.2 us (4%)
  other arithmetic  22.3 us (2%)
  between operations  13.5 us (1%)
    all_gather x1, waiting for transfers between devices, local(): amp_rows = lax.all_gather(amp_local, 'col', axis=1, tiled=True)  641 us
    all_gather x1, waiting for transfers between devices, local(): lax.all_gather(int_local, 'row', axis=0, tiled=True)  155 us
    all_gather x1, local copies, waits for them, and re-layouts, local(): lax.all_gather(int_local, 'row', axis=0, tiled=True)  42.8 us
    dot_general x1, matrix products, local(): jnp.einsum('acik,cbkj->abij', amp_rows, lax.all_gather(int_local, 'row',...  41.2 us
    all_gather x1, local copies, waits for them, and re-layouts, local(): amp_rows = lax.all_gather(amp_local, 'col', axis=1, tiled=True)  34.2 us
    all_to_all x1, blocking collectives, local(): lax.all_to_all(spread.astype(jnp.bfloat16), ('row', 'col'), split_axis=1,...  22.9 us
  transfers between devices with their start and end apart: 3, of which 3 were waited for; matrix products, arithmetic and copies ran while one was open for 4% of the time, Pallas kernels for 0%

commit v1 on v0

v1 whole, which is shorter than its diff:
```python
import functools

import jax
import jax.numpy as jnp
import numpy as np
from jax import lax
from jax.experimental import pallas as pl
from jax.experimental.pallas import tpu as pltpu
from jax.sharding import PartitionSpec as P

OCC = 16
PAIRS = OCC * OCC
BA = 32
BB = 64
LANES = 128
F32, BF16 = jnp.float32, jnp.bfloat16
MESH = pl.DeviceIdType.MESH
VMEM = pl.BlockSpec(memory_space=pltpu.VMEM)
ANY = pl.BlockSpec(memory_space=pl.ANY)
TILES = [(i, jj) for i in range(OCC) for jj in range((i + 1) // 2, OCC // 2)]
NT = len(TILES)


def spread_matrix():
    sel = np.zeros((2, NT, OCC, OCC), np.float32)
    for t, (i, jj) in enumerate(TILES):
        for jp in range(2):
            j = 2 * jj + jp
            if j > i:
                sel[jp, t, i, j] = 1.0
                sel[jp, t, j, i] = -1.0
    sel = sel.reshape(2 * NT, PAIRS)
    return np.concatenate([sel, sel], 0)


def trade_chunks(blocks):
    lane = lax.broadcasted_iota(jnp.int32, blocks[0].shape, 1)
    blocks = list(blocks)
    for d in (4, 2, 1):
        upper = (lane & (16 * d)) != 0
        for c in range(8):
            if c & d:
                continue
            lo, hi = blocks[c], blocks[c + d]
            blocks[c] = jnp.where(upper, pltpu.roll(hi, 16 * d, 1), lo)
            blocks[c + d] = jnp.where(upper, hi, pltpu.roll(lo, LANES - 16 * d, 1))
    return blocks


def arrange_kernel(a_ref, w_ref, at_ref, wt_ref, wide0, wide1):
    wides = (wide0, wide1)
    for h, wide in enumerate(wides):
        wide[...] = a_ref[:, :, h * LANES:(h + 1) * LANES].astype(F32).reshape(BA * BB, LANES)

    def amp(g, _):
        for h, wide in enumerate(wides):
            blocks = [wide[pl.ds(g * 8 + c8, BA, stride=BB), :] for c8 in range(8)]
            for i8, out in enumerate(trade_chunks(blocks)):
                at_ref[lax.rem(g, 4), g // 4, pl.ds((h * 8 + i8) * BA, BA), :] = out.astype(BF16)
        return 0

    lax.fori_loop(0, 8, amp, 0)
    q = lax.broadcasted_iota(jnp.int32, (PAIRS, PAIRS), 0)
    r = lax.broadcasted_iota(jnp.int32, (PAIRS, PAIRS), 1)
    perm = jnp.where(((q >> 4) == (r & 15)) & ((q & 15) == (r >> 4)), 1.0, 0.0).astype(BF16)

    def integ(g, _):
        x = w_ref[pl.ds(g * 8, 8)].reshape(8 * BB, PAIRS)
        y = jnp.dot(x, perm, preferred_element_type=F32)
        for h in range(2):
            for s in range(2):
                blocks = [y[c8 * BB + s * 32:c8 * BB + s * 32 + 32, h * LANES:(h + 1) * LANES] for c8 in range(8)]
                for j8, out in enumerate(trade_chunks(blocks)):
                    wt_ref[g, pl.ds((h * 8 + j8) * BB + s * 32, 32), :] = out.astype(BF16)
        return 0

    lax.fori_loop(0, 4, integ, 0)


def cycle_kernel(at, wt, r_ref, abuf, wbuf, cbuf, dsend, drecv, dsum, xf, xb, ybuf, yf,
                 x_ss, x_rs, g_ss, g_rs, f_ss, f_rs, s_ss, s_rs, sf_ss, sf_rs, d_ss, d_rs, m_ss, m_rs, l_sem):
    row, col = lax.axis_index("row"), lax.axis_index("col")
    z, xh, k = row // 4, lax.rem(row // 2, 2), lax.rem(row, 2)
    y, xl = col // 2, lax.rem(col, 2)
    x = xh * 2 + xl

    def at4(v, s):
        return lax.rem(v + (s + 4), 4)

    def dev(x, y, z, k):
        return (z * 4 + (x // 2) * 2 + k, y * 2 + lax.rem(x, 2))

    x_dev = [dev(at4(x, r), y, z, k) for r in range(4)]
    y_dev = [dev(x, at4(y, 1), z, k), dev(x, at4(y, -1), z, k)]
    z_dev = [dev(x, y, at4(z, 1), k), dev(x, y, at4(z, -1), k)]
    sib = dev(x, y, z, 1 - k)
    turned = xl * 2 + xh
    m_dev = [dev(turned, z, y, k), dev(turned, z, y, 1 - k)]
    own_turned = jnp.logical_and(y == z, xh == xl)

    bar = pltpu.get_barrier_semaphore()
    for d in x_dev[1:] + y_dev + z_dev + [sib, m_dev[1]]:
        pl.semaphore_signal(bar, inc=1, device_id=d, device_id_type=MESH)

    @pl.when(jnp.logical_not(own_turned))
    def _():
        pl.semaphore_signal(bar, inc=1, device_id=m_dev[0], device_id_type=MESH)
        pl.semaphore_wait(bar, 10)

    @pl.when(own_turned)
    def _():
        pl.semaphore_wait(bar, 9)

    def remote(src, dst, ss, rs, to):
        return pltpu.make_async_remote_copy(
            src_ref=src, dst_ref=dst, send_sem=ss, recv_sem=rs, device_id=to, device_id_type=MESH)

    def arrived(ref, ss, rs):
        remote(ref, ref, ss, rs, sib).wait_recv()

    sends = []

    def go(*args):
        copy = remote(*args)
        copy.start()
        sends.append(copy)

    own_a = pltpu.make_async_copy(at.at[x], abuf.at[y, x], l_sem.at[0])
    own_w = pltpu.make_async_copy(wt.at[x], wbuf.at[z, k, x], l_sem.at[1])
    own_a.start()
    own_w.start()
    for r in (1, 3, 2):
        to = at4(x, r)
        go(at.at[to], abuf.at[y, x], x_ss.at[0, r], x_rs.at[0, r], x_dev[r])
        go(wt.at[to], wbuf.at[z, k, x], x_ss.at[1, r], x_rs.at[1, r], x_dev[r])

    def ring(r):
        src = at4(x, -r)
        a_from = at.at[x] if r == 0 else abuf.at[y, src]
        w_from = wt.at[x] if r == 0 else wbuf.at[z, k, src]
        if r:
            arrived(abuf.at[y, src], x_ss.at[0, r], x_rs.at[0, r])
        for d in range(2):
            go(a_from, abuf.at[y, src], g_ss.at[0, d, r], g_rs.at[0, d, r], y_dev[d])
        if r:
            arrived(wbuf.at[z, k, src], x_ss.at[1, r], x_rs.at[1, r])
        for d in range(2):
            go(w_from, wbuf.at[z, k, src], g_ss.at[1, d, r], g_rs.at[1, d, r], z_dev[d])
        go(w_from, wbuf.at[z, k, src], s_ss.at[0, r], s_rs.at[0, r], sib)

    def forward(r):
        src = at4(x, -r)
        for d in range(2):
            yy, zz = at4(y, 2 * d - 1), at4(z, 2 * d - 1)
            arrived(abuf.at[yy, src], g_ss.at[0, d, r], g_rs.at[0, d, r])
            go(abuf.at[yy, src, d], abuf.at[yy, src, d], f_ss.at[0, d, r], f_rs.at[0, d, r], y_dev[d])
            arrived(wbuf.at[zz, k, src], g_ss.at[1, d, r], g_rs.at[1, d, r])
            half = wbuf.at[zz, k, src, pl.ds(d * 512, 512)]
            go(half, half, f_ss.at[1, d, r], f_rs.at[1, d, r], z_dev[d])
            go(wbuf.at[zz, k, src], wbuf.at[zz, k, src], s_ss.at[1 + d, r], s_rs.at[1 + d, r], sib)

    def finish(r):
        src = at4(x, -r)
        yy, zz = at4(y, 2), at4(z, 2)
        for d in range(2):
            arrived(abuf.at[yy, src, d], f_ss.at[0, d, r], f_rs.at[0, d, r])
            half = wbuf.at[zz, k, src, pl.ds(d * 512, 512)]
            arrived(half, f_ss.at[1, d, r], f_rs.at[1, d, r])
            go(half, half, sf_ss.at[d, r], sf_rs.at[d, r], sib)

    ring(0)
    forward(0)
    ring(1)
    ring(3)
    finish(0)
    forward(1)
    ring(2)
    forward(3)
    finish(1)
    forward(2)
    finish(3)
    finish(2)
    own_a.wait()
    own_w.wait()
    for r in range(4):
        src = at4(x, -r)
        arrived(wbuf.at[z, 1 - k, src], s_ss.at[0, r], s_rs.at[0, r])
        for d in range(2):
            zz = at4(z, 2 * d - 1)
            arrived(wbuf.at[zz, 1 - k, src], s_ss.at[1 + d, r], s_rs.at[1 + d, r])
            arrived(wbuf.at[at4(z, 2), 1 - k, src, pl.ds(d * 512, 512)], sf_ss.at[d, r], sf_rs.at[d, r])

    lane = lax.broadcasted_iota(jnp.int32, (BA, LANES), 1)
    left = lane < BB

    def quadrant(s, _):
        to = lax.rem(x + s + 1, 4)
        th, tl = to // 2, lax.rem(to, 2)
        split = [(hi, mid, lo) for hi in range(4) for mid in range(2) for lo in range(2)]

        def columns(n, _):
            lhs = jnp.concatenate([abuf[hi, 2 * th + mid, lo] for hi, mid, lo in split], axis=1)
            rhs = jnp.concatenate([wbuf[hi, lo, 2 * mid + tl, pl.ds(n * 256, 256)] for hi, mid, lo in split], axis=1)
            cbuf[:, pl.ds(pl.multiple_of(n * 256, 256), 256)] = lax.dot_general(
                lhs, rhs, (((1,), (1,)), ((), ())), preferred_element_type=F32)
            return 0

        lax.fori_loop(0, 4, columns, 0)
        for t, (i, jj) in enumerate(TILES):
            ii, ip = i // 2, i % 2
            here = cbuf[i * BA:(i + 1) * BA, jj * LANES:(jj + 1) * LANES]
            even = cbuf[2 * jj * BA:(2 * jj + 1) * BA, ii * LANES:(ii + 1) * LANES]
            odd = cbuf[(2 * jj + 1) * BA:(2 * jj + 2) * BA, ii * LANES:(ii + 1) * LANES]
            if ip == 0:
                other = jnp.where(left, even, pltpu.roll(odd, BB, 1))
            else:
                other = jnp.where(left, pltpu.roll(even, BB, 1), odd)
            tile = here - other
            dsum[t * BA:(t + 1) * BA, :] = tile
            dsend[s, t * BA:(t + 1) * BA, :] = tile.astype(BF16)

        @pl.when(s < 3)
        def _():
            remote(dsend.at[s], drecv.at[s], d_ss.at[s], d_rs.at[s], dev(to, y, z, k)).start()
        return 0

    lax.fori_loop(0, 4, quadrant, 0)
    for s in range(3):
        arrived(drecv.at[s], d_ss.at[s], d_rs.at[s])
    dsum[...] = dsum[...] + drecv[0].astype(F32) + drecv[1].astype(F32) + drecv[2].astype(F32)

    left2 = lax.broadcasted_iota(jnp.int32, (BB, LANES), 1) < BB

    def turn(p, _):
        rows = jnp.concatenate([dsum[pl.ds(2 * p + q, NT, stride=BA), :] for q in range(2)], axis=0)
        t = rows.T
        lo, hi = t[:BB], t[BB:]
        first = jnp.where(left2, lo, pltpu.roll(hi, BB, 1))
        second = jnp.where(left2, pltpu.roll(lo, BB, 1), hi)
        xf[2 * p] = first
        xf[2 * p + 1] = second
        xb[2 * p] = first.astype(BF16)
        xb[2 * p + 1] = second.astype(BF16)
        return 0

    lax.fori_loop(0, BA // 2, turn, 0)
    mine = xb.at[:, pl.ds(pl.multiple_of(k * BA, BA), BA)]
    other = xb.at[:, pl.ds(pl.multiple_of((1 - k) * BA, BA), BA)]
    go(other, ybuf.at[k], m_ss.at[1], m_rs.at[1], m_dev[1])

    @pl.when(own_turned)
    def _():
        copy = pltpu.make_async_copy(mine, ybuf.at[k], l_sem.at[2])
        copy.start()
        copy.wait()

    @pl.when(jnp.logical_not(own_turned))
    def _():
        copy = remote(mine, ybuf.at[k], m_ss.at[0], m_rs.at[0], m_dev[0])
        copy.start()
        copy.wait()

    arrived(ybuf.at[1 - k], m_ss.at[1], m_rs.at[1])
    yf[...] = ybuf[...].astype(F32).reshape(2 * BA * BA, LANES)

    def mirror(a, _):
        r_ref[a] = xf[a] - yf[pl.ds(a, BB, stride=BA), :]
        return 0

    lax.fori_loop(0, BA, mirror, 0)
    for copy in sends:
        copy.wait_send()
    for s in range(3):
        remote(dsend.at[s], drecv.at[s], d_ss.at[s], d_rs.at[s], sib).wait_send()


STEP = 8


def update_kernel(a_ref, r_ref, sel_ref, occ_ref, vrow_ref, vcol_ref, o_ref):
    r = r_ref[...].reshape(STEP * BB, LANES)
    hi = r.astype(BF16)
    lo = (r - hi.astype(F32)).astype(BF16)
    full = jnp.dot(jnp.concatenate([hi, lo], axis=1), sel_ref[...], preferred_element_type=F32)
    den = (occ_ref[...][None] - vrow_ref[...]) - vcol_ref[...][None]
    o_ref[...] = a_ref[...].astype(F32) + full.reshape(STEP, BB, PAIRS) / den


def local(amplitudes, integrals, occ_energy, vir_energy):
    at, wt = pl.pallas_call(
        arrange_kernel,
        out_shape=(jax.ShapeDtypeStruct((4, 2, 512, LANES), BF16), jax.ShapeDtypeStruct((4, 1024, LANES), BF16)),
        in_specs=[VMEM, VMEM],
        out_specs=(VMEM, VMEM),
        scratch_shapes=[pltpu.VMEM((BA * BB, LANES), F32)] * 2,
        compiler_params=pltpu.CompilerParams(vmem_limit_bytes=40 << 20),
        name="arrange",
    )(amplitudes, integrals)
    dma = pltpu.SemaphoreType.DMA
    resid = pl.pallas_call(
        cycle_kernel,
        out_shape=jax.ShapeDtypeStruct((BA, BB, LANES), F32),
        in_specs=[ANY, ANY],
        out_specs=VMEM,
        scratch_shapes=[
            pltpu.VMEM((4, 4, 2, 512, LANES), BF16),
            pltpu.VMEM((4, 2, 4, 1024, LANES), BF16),
            pltpu.VMEM((512, 1024), F32),
            pltpu.VMEM((4, NT * BA, LANES), BF16),
            pltpu.VMEM((3, NT * BA, LANES), BF16),
            pltpu.VMEM((NT * BA, LANES), F32),
            pltpu.VMEM((BA, BB, LANES), F32),
            pltpu.VMEM((BA, BB, LANES), BF16),
            pltpu.VMEM((2, BA, BA, LANES), BF16),
            pltpu.VMEM((2 * BA * BA, LANES), F32),
            dma((2, 4)), dma((2, 4)), dma((2, 2, 4)), dma((2, 2, 4)), dma((2, 2, 4)), dma((2, 2, 4)),
            dma((3, 4)), dma((3, 4)), dma((2, 4)), dma((2, 4)), dma((3,)), dma((3,)), dma((2,)), dma((2,)), dma((3,)),
        ],
        compiler_params=pltpu.CompilerParams(collective_id=0, has_side_effects=True, vmem_limit_bytes=48 << 20),
        name="cycle",
    )(at, wt)
    row_pos, col_pos = lax.axis_index("row"), lax.axis_index("col")
    vir_rows = lax.dynamic_slice_in_dim(vir_energy, row_pos * BA, BA).reshape(BA, 1, 1)
    vir_cols = lax.dynamic_slice_in_dim(vir_energy, col_pos * BB, BB).reshape(BB, 1)
    occ = (occ_energy[:, None] + occ_energy[None, :]).reshape(1, PAIRS)
    sel = jnp.asarray(spread_matrix(), BF16)
    return pl.pallas_call(
        update_kernel,
        grid=(BA // STEP,),
        out_shape=jax.ShapeDtypeStruct((BA, BB, PAIRS), F32),
        in_specs=[
            pl.BlockSpec((STEP, BB, PAIRS), lambda s: (s, 0, 0)),
            pl.BlockSpec((STEP, BB, LANES), lambda s: (s, 0, 0)),
            pl.BlockSpec((2 * LANES, PAIRS), lambda s: (0, 0)),
            pl.BlockSpec((1, PAIRS), lambda s: (0, 0)),
            pl.BlockSpec((STEP, 1, 1), lambda s: (s, 0, 0)),
            pl.BlockSpec((BB, 1), lambda s: (0, 0)),
        ],
        out_specs=pl.BlockSpec((STEP, BB, PAIRS), lambda s: (s, 0, 0)),
        compiler_params=pltpu.CompilerParams(vmem_limit_bytes=40 << 20),
        name="update",
    )(amplitudes, resid, sel, occ, vir_rows, vir_cols)


def solution(mesh):
    placed = (P("row", "col", None), P("row", "col", None), P(), P())
    return jax.shard_map(
        local, mesh=mesh, in_specs=placed, out_specs=P("row", "col", None), check_vma=False
    )
```

time: 1040 us -> 129 us (0.12)
  the two profiles are of different devices: /device:TPU:11 before, /device:TPU:33 now
where the time goes in v1:
time: 129 us
  Pallas kernels  125 us (97%)
  local copies, waits for them, and re-layouts  3.56 us (3%)
    pallas_call x1, Pallas kernels, local(): pl.pallas_call(cycle_kernel, out_shape=jax.ShapeDtypeStruct((BA, BB, LANE...  117 us
    pallas_call x1, Pallas kernels, local(): pl.pallas_call(arrange_kernel, out_shape=(jax.ShapeDtypeStruct((4, 2, 512...  5 us
    unnamed x10, local copies, waits for them, and re-layouts  3.15 us

profile of v1, /device:TPU:33, one launch (start us, length us, event | category | flops | bytes accessed | tf_op | source)
XLA Modules:
  0.0 129.1 jit_solution(2301198929816234195)
XLA Ops:
  0.0 0.0 copy-start
  0.0 0.7 copy-done
  0.7 0.1 dynamic-slice_bitcast_fusion
  0.8 0.1 dynamic-slice_bitcast_fusion.1
  0.8 0.8 broadcast_add_fusion
  1.6 0.1 add.32.occ_ref
  1.7 0.1 copy.6.vrow_ref
  1.8 0.1 copy.7.vcol_ref
  1.9 0.0 copy-start.1
  1.9 1.2 copy-done.1
  3.1 0.0 copy-start.3
  3.1 1.2 copy-done.3
  4.4 5.0 %arrange.1 = (bf16[4,2,512,128]{3,2,1,0:T(8,128)(2,1)S(1)}, bf16[4,1024,128]{2,1,0:T(8,128)(2,1)S(1)}) custom-call(bf16[32,64,256]{2,1,0:T(8,128)(2,1)S(1)} %copy-done.1, bf16[32,64,256]{2,1,0:T(8,128)(2,1)S(1)} %copy-done.3), custom_call_target="tpu_custom_call" | custom-call | tf_op jit(solution)/shard_map/arrange/pallas_call | solution.py:290
  9.4 0.0 copy-start.2
  9.4 0.0 copy-start.4
  9.4 117.3 %cycle.1.r_ref = f32[32,64,128]{2,1,0:T(8,128)S(1)} custom-call(bf16[4,2,512,128]{3,2,1,0:T(8,128)(2,1)S(1)} %get-tuple-element.7.at, bf16[4,1024,128]{2,1,0:T(8,128)(2,1)S(1)} %get-tuple-element.8.wt), custom_call_target="tpu_custom_call" | custom-call | tf_op jit(solution)/shard_map/cycle/pallas_call | solution.py:300
  126.7 0.0 copy-done.2
  126.7 0.0 copy-done.4
  126.7 2.4 %update.1 = f32[32,64,256]{2,1,0:T(8,128)} custom-call(bf16[32,64,256]{2,1,0:T(8,128)(2,1)S(1)} %copy-done.2, f32[32,64,128]{2,1,0:T(8,128)S(1)} %cycle.1.r_ref, bf16[256,256]{1,0:T(8,128)(2,1)S(1)} %copy-done.4, f32[1,256]{1,0:T(1,128)S(1)} %add.32.occ_ref, f32[32,1,1]{2,1,0:T(1,128)S(1)} %copy.6.vrow_ref, f32[64,1]{1,0:T(8,128)S(1)} %copy.7.vcol_ref), custom_call_target="tpu_custom_call" | custom-call | tf_op jit(solution)/shard_map/update/pallas_call | solution.py:327
Async XLA Ops:
  0.0 0.7 copy-start
  1.9 1.2 copy-start.1
  3.1 1.2 copy-start.3
  9.4 117.4 %copy-start.2 = (bf16[32,64,256]{2,1,0:T(8,128)(2,1)S(1)}, bf16[32,64,256]{2,1,0:T(8,128)(2,1)}, u32[]{:S(2)}) copy-start(bf16[32,64,256]{2,1,0:T(8,128)(2,1)} %a_ref.3) | copy-start | bytes 3145732
  9.4 117.4 %copy-start.4 = (bf16[256,256]{1,0:T(8,128)(2,1)S(1)}, bf16[256,256]{1,0:T(8,128)(2,1)}, u32[]{:S(2)}) copy-start(bf16[256,256]{1,0:T(8,128)(2,1)} %constant.19.clone.sel_ref) | copy-start | bytes 393220

commit v2 on v1

v2 whole, which is shorter than its diff:
```python
import functools

import jax
import jax.numpy as jnp
import numpy as np
from jax import lax
from jax.experimental import pallas as pl
from jax.experimental.pallas import tpu as pltpu
from jax.sharding import PartitionSpec as P

OCC = 16
PAIRS = OCC * OCC
BA = 32
BB = 64
LANES = 128
F32, BF16 = jnp.float32, jnp.bfloat16
MESH = pl.DeviceIdType.MESH
VMEM = pl.BlockSpec(memory_space=pltpu.VMEM)
ANY = pl.BlockSpec(memory_space=pl.ANY)
TILES = [(i, jj) for i in range(OCC) for jj in range((i + 1) // 2, OCC // 2)]
NT = len(TILES)


def spread_matrix():
    sel = np.zeros((2, NT, OCC, OCC), np.float32)
    for t, (i, jj) in enumerate(TILES):
        for jp in range(2):
            j = 2 * jj + jp
            if j > i:
                sel[jp, t, i, j] = 1.0
                sel[jp, t, j, i] = -1.0
    sel = sel.reshape(2 * NT, PAIRS)
    return np.concatenate([sel, sel], 0)


def trade_chunks(blocks):
    lane = lax.broadcasted_iota(jnp.int32, blocks[0].shape, 1)
    blocks = list(blocks)
    for d in (4, 2, 1):
        upper = (lane & (16 * d)) != 0
        for c in range(8):
            if c & d:
                continue
            lo, hi = blocks[c], blocks[c + d]
            blocks[c] = jnp.where(upper, pltpu.roll(hi, 16 * d, 1), lo)
            blocks[c + d] = jnp.where(upper, hi, pltpu.roll(lo, LANES - 16 * d, 1))
    return blocks


def cycle_kernel(a_hbm, w_hbm, r_ref, av, wv, wide0, wide1, atb, wtb, abuf, wbuf, cbuf, dsend, drecv, dsum, xf, xb, ybuf, yf,
                 x_ss, x_rs, g_ss, g_rs, f_ss, f_rs, s_ss, s_rs, sf_ss, sf_rs, d_ss, d_rs, m_ss, m_rs, l_sem):
    row, col = lax.axis_index("row"), lax.axis_index("col")
    z, xh, k = row // 4, lax.rem(row // 2, 2), lax.rem(row, 2)
    y, xl = col // 2, lax.rem(col, 2)
    x = xh * 2 + xl

    def at4(v, s):
        return lax.rem(v + (s + 4), 4)

    def dev(x, y, z, k):
        return (z * 4 + (x // 2) * 2 + k, y * 2 + lax.rem(x, 2))

    x_dev = [dev(at4(x, r), y, z, k) for r in range(4)]
    y_dev = [dev(x, at4(y, 1), z, k), dev(x, at4(y, -1), z, k)]
    z_dev = [dev(x, y, at4(z, 1), k), dev(x, y, at4(z, -1), k)]
    sib = dev(x, y, z, 1 - k)
    turned = xl * 2 + xh
    m_dev = [dev(turned, z, y, k), dev(turned, z, y, 1 - k)]
    own_turned = jnp.logical_and(y == z, xh == xl)

    bar = pltpu.get_barrier_semaphore()
    for d in x_dev[1:] + y_dev + z_dev + [sib, m_dev[1]]:
        pl.semaphore_signal(bar, inc=1, device_id=d, device_id_type=MESH)

    @pl.when(jnp.logical_not(own_turned))
    def _():
        pl.semaphore_signal(bar, inc=1, device_id=m_dev[0], device_id_type=MESH)

    load_a = pltpu.make_async_copy(a_hbm, av, l_sem.at[0])
    load_w = pltpu.make_async_copy(w_hbm, wv, l_sem.at[1])
    load_w.start()
    load_a.start()

    def remote(src, dst, ss, rs, to):
        return pltpu.make_async_remote_copy(
            src_ref=src, dst_ref=dst, send_sem=ss, recv_sem=rs, device_id=to, device_id_type=MESH)

    def arrived(ref, ss, rs):
        remote(ref, ref, ss, rs, sib).wait_recv()

    sends = []

    def go(*args):
        copy = remote(*args)
        copy.start()
        sends.append(copy)

    q = lax.broadcasted_iota(jnp.int32, (PAIRS, PAIRS), 0)
    r = lax.broadcasted_iota(jnp.int32, (PAIRS, PAIRS), 1)
    perm = jnp.where(((q >> 4) == (r & 15)) & ((q & 15) == (r >> 4)), 1.0, 0.0).astype(BF16)

    def arrange_w(share, out):
        wp = jnp.dot(wv[pl.ds(share * 8, 8)].reshape(8 * BB, PAIRS), perm, preferred_element_type=F32)
        for h in range(2):
            for s in range(2):
                blocks = [wp[c8 * BB + s * 32:c8 * BB + s * 32 + 32, h * LANES:(h + 1) * LANES] for c8 in range(8)]
                for j8, v in enumerate(trade_chunks(blocks)):
                    at = (h * 8 + j8) * BB + s * 32
                    out[at:at + 32, :] = v.astype(BF16)

    def arrange_a(share, out):
        for lo in range(2):
            for h, wide in enumerate((wide0, wide1)):
                blocks = [wide[pl.ds((share + 4 * lo) * 8 + c8, BA, stride=BB), :] for c8 in range(8)]
                for i8, v in enumerate(trade_chunks(blocks)):
                    at = (h * 8 + i8) * 16
                    v = v.astype(BF16)
                    out[lo, at:at + 16, :] = v[:16]
                    out[lo, 256 + at:256 + at + 16, :] = v[16:]

    load_w.wait()
    arrange_w(x, wbuf.at[z, k, x])

    @pl.when(own_turned)
    def _():
        pl.semaphore_wait(bar, 9)

    @pl.when(jnp.logical_not(own_turned))
    def _():
        pl.semaphore_wait(bar, 10)

    def ring_w(r):
        src = at4(x, -r)
        if r:
            arrived(wbuf.at[z, k, src], x_ss.at[1, r], x_rs.at[1, r])
        for d in range(2):
            go(wbuf.at[z, k, src], wbuf.at[z, k, src], g_ss.at[1, d, r], g_rs.at[1, d, r], z_dev[d])
        go(wbuf.at[z, k, src], wbuf.at[z, k, src], s_ss.at[0, r], s_rs.at[0, r], sib)

    def ring_a(r):
        src = at4(x, -r)
        if r:
            arrived(abuf.at[y, src], x_ss.at[0, r], x_rs.at[0, r])
        for d in range(2):
            go(abuf.at[y, src], abuf.at[y, src], g_ss.at[0, d, r], g_rs.at[0, d, r], y_dev[d])

    ring_w(0)
    load_a.wait()
    for h, wide in enumerate((wide0, wide1)):
        wide[...] = av[:, :, h * LANES:(h + 1) * LANES].astype(F32).reshape(BA * BB, LANES)
    arrange_a(x, abuf.at[y, x])
    ring_a(0)

    def share_out(n, _):
        r = (1 + 2 * n) - 3 * (n // 2)
        to = at4(x, r)
        there = dev(to, y, z, k)
        arrange_w(to, wtb.at[n])
        remote(wtb.at[n], wbuf.at[z, k, x], x_ss.at[1, r], x_rs.at[1, r], there).start()
        arrange_a(to, atb.at[n])
        remote(atb.at[n], abuf.at[y, x], x_ss.at[0, r], x_rs.at[0, r], there).start()
        return 0

    lax.fori_loop(0, 3, share_out, 0)

    def forward(r):
        src = at4(x, -r)
        for d in range(2):
            yy, zz = at4(y, 2 * d - 1), at4(z, 2 * d - 1)
            arrived(wbuf.at[zz, k, src], g_ss.at[1, d, r], g_rs.at[1, d, r])
            half = wbuf.at[zz, k, src, pl.ds(d * 512, 512)]
            go(half, half, f_ss.at[1, d, r], f_rs.at[1, d, r], z_dev[d])
            go(wbuf.at[zz, k, src], wbuf.at[zz, k, src], s_ss.at[1 + d, r], s_rs.at[1 + d, r], sib)
            arrived(abuf.at[yy, src], g_ss.at[0, d, r], g_rs.at[0, d, r])
            go(abuf.at[yy, src, d], abuf.at[yy, src, d], f_ss.at[0, d, r], f_rs.at[0, d, r], y_dev[d])

    def finish(r):
        src = at4(x, -r)
        yy, zz = at4(y, 2), at4(z, 2)
        for d in range(2):
            half = wbuf.at[zz, k, src, pl.ds(d * 512, 512)]
            arrived(half, f_ss.at[1, d, r], f_rs.at[1, d, r])
            go(half, half, sf_ss.at[d, r], sf_rs.at[d, r], sib)
            arrived(abuf.at[yy, src, d], f_ss.at[0, d, r], f_rs.at[0, d, r])

    forward(0)
    ring_w(1)
    ring_a(1)
    ring_w(3)
    ring_a(3)
    finish(0)
    forward(1)
    ring_w(2)
    ring_a(2)
    forward(3)
    finish(1)
    forward(2)
    finish(3)
    finish(2)
    for r in range(4):
        src = at4(x, -r)
        arrived(wbuf.at[z, 1 - k, src], s_ss.at[0, r], s_rs.at[0, r])
        for d in range(2):
            zz = at4(z, 2 * d - 1)
            arrived(wbuf.at[zz, 1 - k, src], s_ss.at[1 + d, r], s_rs.at[1 + d, r])
            arrived(wbuf.at[at4(z, 2), 1 - k, src, pl.ds(d * 512, 512)], sf_ss.at[d, r], sf_rs.at[d, r])

    left = lax.broadcasted_iota(jnp.int32, (16, LANES), 1) < BB

    def quadrant(n, _):
        h, s = n // 4, lax.rem(n, 4)
        to = lax.rem(x + s + 1, 4)
        th, tl = to // 2, lax.rem(to, 2)
        split = [(hi, mid, lo) for hi in range(4) for mid in range(2) for lo in range(2)]

        def columns(n, _):
            rows = pl.ds(pl.multiple_of(h * 256, 256), 256)
            lhs = jnp.concatenate([abuf[hi, 2 * th + mid, lo, rows] for hi, mid, lo in split], axis=1)
            rhs = jnp.concatenate([wbuf[hi, lo, 2 * mid + tl, pl.ds(n * 512, 512)] for hi, mid, lo in split], axis=1)
            cbuf[:, pl.ds(pl.multiple_of(n * 512, 512), 512)] = lax.dot_general(
                lhs, rhs, (((1,), (1,)), ((), ())), preferred_element_type=F32)
            return 0

        lax.fori_loop(0, 2, columns, 0)
        for t, (i, jj) in enumerate(TILES):
            ii, ip = i // 2, i % 2
            here = cbuf[i * 16:(i + 1) * 16, jj * LANES:(jj + 1) * LANES]
            even = cbuf[2 * jj * 16:(2 * jj + 1) * 16, ii * LANES:(ii + 1) * LANES]
            odd = cbuf[(2 * jj + 1) * 16:(2 * jj + 2) * 16, ii * LANES:(ii + 1) * LANES]
            if ip == 0:
                other = jnp.where(left, even, pltpu.roll(odd, BB, 1))
            else:
                other = jnp.where(left, pltpu.roll(even, BB, 1), odd)
            tile = here - other
            dsum[pl.ds(h * (NT * 16) + t * 16, 16), :] = tile
            dsend[n, t * 16:(t + 1) * 16, :] = tile.astype(BF16)

        @pl.when(s < 3)
        def _():
            remote(dsend.at[n], drecv.at[n], d_ss.at[n], d_rs.at[n], dev(to, y, z, k)).start()
        return 0

    lax.fori_loop(0, 8, quadrant, 0)

    left2 = lax.broadcasted_iota(jnp.int32, (BB, LANES), 1) < BB
    b_mine = pl.ds(pl.multiple_of(k * BA, BA), BA)
    b_other = pl.ds(pl.multiple_of((1 - k) * BA, BA), BA)
    for h in range(2):
        for s in range(3):
            arrived(drecv.at[4 * h + s], d_ss.at[4 * h + s], d_rs.at[4 * h + s])
        part = pl.ds(h * NT * 16, NT * 16)
        dsum[part, :] = (dsum[part, :] + drecv[4 * h].astype(F32) + drecv[4 * h + 1].astype(F32)
                         + drecv[4 * h + 2].astype(F32))

        def turn(p, _):
            rows = jnp.concatenate(
                [dsum[pl.ds(h * NT * 16 + 2 * p + q, NT, stride=16), :] for q in range(2)], axis=0)
            t = rows.T
            lo, hi = t[:BB], t[BB:]
            first = jnp.where(left2, lo, pltpu.roll(hi, BB, 1))
            second = jnp.where(left2, pltpu.roll(lo, BB, 1), hi)
            at = h * 16 + 2 * p
            xf[at] = first
            xf[at + 1] = second
            xb[at] = first.astype(BF16)
            xb[at + 1] = second.astype(BF16)
            return 0

        lax.fori_loop(0, 8, turn, 0)
        a_part = pl.ds(h * 16, 16)
        go(xb.at[a_part, b_other], ybuf.at[k, a_part], m_ss.at[1, h], m_rs.at[1, h], m_dev[1])
        same = (xb.at[a_part, b_mine], ybuf.at[k, a_part])

        @pl.when(own_turned)
        def _():
            pltpu.make_async_copy(*same, l_sem.at[2 + h]).start()

        @pl.when(jnp.logical_not(own_turned))
        def _():
            remote(*same, m_ss.at[0, h], m_rs.at[0, h], m_dev[0]).start()

    for h in range(2):
        a_part = pl.ds(h * 16, 16)
        same = (xb.at[a_part, b_mine], ybuf.at[k, a_part])

        @pl.when(own_turned)
        def _():
            pltpu.make_async_copy(*same, l_sem.at[2 + h]).wait()

        @pl.when(jnp.logical_not(own_turned))
        def _():
            remote(*same, m_ss.at[0, h], m_rs.at[0, h], m_dev[0]).wait()

        arrived(ybuf.at[1 - k, a_part], m_ss.at[1, h], m_rs.at[1, h])
        for c in range(2):
            at = c * BA * BA + h * 16 * BA
            yf[at:at + 16 * BA, :] = ybuf[c, h * 16:h * 16 + 16].astype(F32).reshape(16 * BA, LANES)

    def mirror(a, _):
        r_ref[a] = xf[a] - yf[pl.ds(a, BB, stride=BA), :]
        return 0

    lax.fori_loop(0, BA, mirror, 0)
    for copy in sends:
        copy.wait_send()
    for n, r in enumerate((1, 3, 2)):
        remote(wtb.at[n], wbuf.at[z, k, x], x_ss.at[1, r], x_rs.at[1, r], sib).wait_send()
        remote(atb.at[n], abuf.at[y, x], x_ss.at[0, r], x_rs.at[0, r], sib).wait_send()
    for h in range(2):
        for s in range(3):
            n = 4 * h + s
            remote(dsend.at[n], drecv.at[n], d_ss.at[n], d_rs.at[n], sib).wait_send()


STEP = 8


def update_kernel(a_ref, r_ref, sel_ref, occ_ref, vrow_ref, vcol_ref, o_ref):
    r = r_ref[...].reshape(STEP * BB, LANES)
    hi = r.astype(BF16)
    lo = (r - hi.astype(F32)).astype(BF16)
    full = jnp.dot(jnp.concatenate([hi, lo], axis=1), sel_ref[...], preferred_element_type=F32)
    den = (occ_ref[...][None] - vrow_ref[...]) - vcol_ref[...][None]
    o_ref[...] = a_ref[...].astype(F32) + full.reshape(STEP, BB, PAIRS) / den


def local(amplitudes, integrals, occ_energy, vir_energy):
    dma = pltpu.SemaphoreType.DMA
    resid = pl.pallas_call(
        cycle_kernel,
        out_shape=jax.ShapeDtypeStruct((BA, BB, LANES), F32),
        in_specs=[ANY, ANY],
        out_specs=VMEM,
        scratch_shapes=[
            pltpu.VMEM((BA, BB, PAIRS), BF16),
            pltpu.VMEM((BA, BB, PAIRS), BF16),
            pltpu.VMEM((BA * BB, LANES), F32),
            pltpu.VMEM((BA * BB, LANES), F32),
            pltpu.VMEM((3, 2, 512, LANES), BF16),
            pltpu.VMEM((3, 1024, LANES), BF16),
            pltpu.VMEM((4, 4, 2, 512, LANES), BF16),
            pltpu.VMEM((4, 2, 4, 1024, LANES), BF16),
            pltpu.VMEM((256, 1024), F32),
            pltpu.VMEM((8, NT * 16, LANES), BF16),
            pltpu.VMEM((8, NT * 16, LANES), BF16),
            pltpu.VMEM((NT * BA, LANES), F32),
            pltpu.VMEM((BA, BB, LANES), F32),
            pltpu.VMEM((BA, BB, LANES), BF16),
            pltpu.VMEM((2, BA, BA, LANES), BF16),
            pltpu.VMEM((2 * BA * BA, LANES), F32),
            dma((2, 4)), dma((2, 4)), dma((2, 2, 4)), dma((2, 2, 4)), dma((2, 2, 4)), dma((2, 2, 4)),
            dma((3, 4)), dma((3, 4)), dma((2, 4)), dma((2, 4)), dma((8,)), dma((8,)), dma((2, 2)), dma((2, 2)), dma((4,)),
        ],
        compiler_params=pltpu.CompilerParams(collective_id=0, has_side_effects=True, vmem_limit_bytes=48 << 20),
        name="cycle",
    )(amplitudes, integrals)
    row_pos, col_pos = lax.axis_index("row"), lax.axis_index("col")
    vir_rows = lax.dynamic_slice_in_dim(vir_energy, row_pos * BA, BA).reshape(BA, 1, 1)
    vir_cols = lax.dynamic_slice_in_dim(vir_energy, col_pos * BB, BB).reshape(BB, 1)
    occ = (occ_energy[:, None] + occ_energy[None, :]).reshape(1, PAIRS)
    sel = jnp.asarray(spread_matrix(), BF16)
    return pl.pallas_call(
        update_kernel,
        grid=(BA // STEP,),
        out_shape=jax.ShapeDtypeStruct((BA, BB, PAIRS), F32),
        in_specs=[
            pl.BlockSpec((STEP, BB, PAIRS), lambda s: (s, 0, 0)),
            pl.BlockSpec((STEP, BB, LANES), lambda s: (s, 0, 0)),
            pl.BlockSpec((2 * LANES, PAIRS), lambda s: (0, 0)),
            pl.BlockSpec((1, PAIRS), lambda s: (0, 0)),
            pl.BlockSpec((STEP, 1, 1), lambda s: (s, 0, 0)),
            pl.BlockSpec((BB, 1), lambda s: (0, 0)),
        ],
        out_specs=pl.BlockSpec((STEP, BB, PAIRS), lambda s: (s, 0, 0)),
        compiler_params=pltpu.CompilerParams(vmem_limit_bytes=40 << 20),
        name="update",
    )(amplitudes, resid, sel, occ, vir_rows, vir_cols)


def solution(mesh):
    placed = (P("row", "col", None), P("row", "col", None), P(), P())
    return jax.shard_map(
        local, mesh=mesh, in_specs=placed, out_specs=P("row", "col", None), check_vma=False
    )
```

time: 129 us -> 113 us (0.88)
  the two profiles are of different devices: /device:TPU:33 before, /device:TPU:11 now
where the time goes in v2:
time: 113 us
  Pallas kernels  109 us (96%)
  local copies, waits for them, and re-layouts  3.55 us (3%)
    pallas_call x1, Pallas kernels, local(): pl.pallas_call(cycle_kernel, out_shape=jax.ShapeDtypeStruct((BA, BB, LANE...  106 us
    unnamed x8, local copies, waits for them, and re-layouts  3.14 us
    pallas_call x1, Pallas kernels, local(): pl.pallas_call(update_kernel, grid=(BA // STEP,), out_shape=jax.ShapeDtyp...  2.36 us

profile of v2, /device:TPU:11, one launch (start us, length us, event | category | flops | bytes accessed | tf_op | source)
XLA Modules:
  0.0 113.2 jit_solution(2564436702517023514)
XLA Ops:
  0.0 0.0 copy-start
  0.0 0.7 copy-done
  0.7 0.1 dynamic-slice_bitcast_fusion
  0.8 0.1 dynamic-slice_bitcast_fusion.1
  0.8 0.8 broadcast_add_fusion
  1.6 0.1 add.32.occ_ref
  1.7 0.1 copy.6.vrow_ref
  1.8 0.1 copy.7.vcol_ref
  1.9 0.0 copy-start.1
  1.9 1.2 %copy-done.1 = bf16[32,64,256]{2,1,0:T(8,128)(2,1)S(1)} copy-done((bf16[32,64,256]{2,1,0:T(8,128)(2,1)S(1)}, bf16[32,64,256]{2,1,0:T(8,128)(2,1)}, u32[]{:S(2)}) %copy-start.1) | copy-done | bytes 1048600
  3.1 0.0 copy-start.2
  3.1 1.2 %copy-done.2 = bf16[32,64,256]{2,1,0:T(8,128)(2,1)S(1)} copy-done((bf16[32,64,256]{2,1,0:T(8,128)(2,1)S(1)}, bf16[32,64,256]{2,1,0:T(8,128)(2,1)}, u32[]{:S(2)}) %copy-start.2) | copy-done | bytes 1048600
  4.4 0.0 copy-start.3
  4.4 106.5 %cycle.1.r_ref = f32[32,64,128]{2,1,0:T(8,128)S(1)} custom-call(bf16[32,64,256]{2,1,0:T(8,128)(2,1)S(1)} %copy-done.1, bf16[32,64,256]{2,1,0:T(8,128)(2,1)S(1)} %copy-done.2), custom_call_target="tpu_custom_call" | custom-call | tf_op jit(solution)/shard_map/cycle/pallas_call | solution.py:329
  110.8 0.0 copy-done.3
  110.8 2.4 %update.1 = f32[32,64,256]{2,1,0:T(8,128)} custom-call(bf16[32,64,256]{2,1,0:T(8,128)(2,1)S(1)} %copy-done.1, f32[32,64,128]{2,1,0:T(8,128)S(1)} %cycle.1.r_ref, bf16[256,256]{1,0:T(8,128)(2,1)S(1)} %copy-done.3, f32[1,256]{1,0:T(1,128)S(1)} %add.32.occ_ref, f32[32,1,1]{2,1,0:T(1,128)S(1)} %copy.6.vrow_ref, f32[64,1]{1,0:T(8,128)S(1)} %copy.7.vcol_ref), custom_call_target="tpu_custom_call" | custom-call | tf_op jit(solution)/shard_map/update/pallas_call | solution.py:362
Async XLA Ops:
  0.0 0.7 copy-start
  1.9 1.2 %copy-start.1 = (bf16[32,64,256]{2,1,0:T(8,128)(2,1)S(1)}, bf16[32,64,256]{2,1,0:T(8,128)(2,1)}, u32[]{:S(2)}) copy-start(bf16[32,64,256]{2,1,0:T(8,128)(2,1)} %a_ref.1) | copy-start | bytes 3145732
  3.1 1.2 %copy-start.2 = (bf16[32,64,256]{2,1,0:T(8,128)(2,1)S(1)}, bf16[32,64,256]{2,1,0:T(8,128)(2,1)}, u32[]{:S(2)}) copy-start(bf16[32,64,256]{2,1,0:T(8,128)(2,1)} %w_hbm.1) | copy-start | bytes 3145732
  4.4 106.5 %copy-start.3 = (bf16[256,256]{1,0:T(8,128)(2,1)S(1)}, bf16[256,256]{1,0:T(8,128)(2,1)}, u32[]{:S(2)}) copy-start(bf16[256,256]{1,0:T(8,128)(2,1)} %constant.19.clone.sel_ref) | copy-start | bytes 393220

commit v3 on v2

--- a/solution.py
+++ b/solution.py
@@ -19,6 +19,7 @@
 ANY = pl.BlockSpec(memory_space=pl.ANY)
 TILES = [(i, jj) for i in range(OCC) for jj in range((i + 1) // 2, OCC // 2)]
 NT = len(TILES)
+ROWS = NT * 8
 
 
 def spread_matrix():
@@ -47,8 +48,8 @@
     return blocks
 
 
-def cycle_kernel(a_hbm, w_hbm, r_ref, av, wv, wide0, wide1, atb, wtb, abuf, wbuf, cbuf, dsend, drecv, dsum, xf, xb, ybuf, yf,
-                 x_ss, x_rs, g_ss, g_rs, f_ss, f_rs, s_ss, s_rs, sf_ss, sf_rs, d_ss, d_rs, m_ss, m_rs, l_sem):
+def cycle_kernel(a_hbm, w_hbm, r_ref, av, wv, wide0, wide1, atb, wtb, ra, rw, rd, abuf, wbuf, cbuf, dsend, drecv, dsum, xf, xb, mid, ybuf, yf,
+                 x_ss, x_rs, xf_ss, xf_rs, g_ss, g_rs, f_ss, f_rs, s_ss, s_rs, sf_ss, sf_rs, d_ss, d_rs, e_ss, e_rs, p_ss, m_ss, m_rs, l_sem):
     row, col = lax.axis_index("row"), lax.axis_index("col")
     z, xh, k = row // 4, lax.rem(row // 2, 2), lax.rem(row, 2)
     y, xl = col // 2, lax.rem(col, 2)
@@ -66,15 +67,33 @@
     sib = dev(x, y, z, 1 - k)
     turned = xl * 2 + xh
     m_dev = [dev(turned, z, y, k), dev(turned, z, y, 1 - k)]
-    own_turned = jnp.logical_and(y == z, xh == xl)
+    diagonal = y == z
+    own_turned = jnp.logical_and(diagonal, xh == xl)
 
     bar = pltpu.get_barrier_semaphore()
-    for d in x_dev[1:] + y_dev + z_dev + [sib, m_dev[1]]:
+
+    def greet(d):
         pl.semaphore_signal(bar, inc=1, device_id=d, device_id_type=MESH)
 
-    @pl.when(jnp.logical_not(own_turned))
+    for d in x_dev[1:] + y_dev + z_dev + [sib]:
+        greet(d)
+
+    @pl.when(diagonal)
     def _():
-        pl.semaphore_signal(bar, inc=1, device_id=m_dev[0], device_id_type=MESH)
+        greet(m_dev[1])
+        for j in range(1, 4):
+            for d in (dev(turned, at4(y, j), z, k), dev(turned, y, at4(z, j), 1 - k),
+                      dev(x, y, at4(z, j), k), dev(x, at4(y, j), z, k)):
+                greet(d)
+
+        @pl.when(jnp.logical_not(own_turned))
+        def _():
+            greet(m_dev[0])
+
+    @pl.when(jnp.logical_not(diagonal))
+    def _():
+        for d in (dev(turned, z, z, k), dev(turned, y, y, 1 - k), dev(x, y, y, k), dev(x, z, z, k)):
+            greet(d)
 
     load_a = pltpu.make_async_copy(a_hbm, av, l_sem.at[0])
     load_w = pltpu.make_async_copy(w_hbm, wv, l_sem.at[1])
@@ -121,17 +140,25 @@
     load_w.wait()
     arrange_w(x, wbuf.at[z, k, x])
 
+    @pl.when(jnp.logical_not(diagonal))
+    def _():
+        pl.semaphore_wait(bar, 12)
+
     @pl.when(own_turned)
     def _():
-        pl.semaphore_wait(bar, 9)
-
-    @pl.when(jnp.logical_not(own_turned))
+        pl.semaphore_wait(bar, 21)
+
+    @pl.when(jnp.logical_and(diagonal, xh != xl))
     def _():
-        pl.semaphore_wait(bar, 10)
+        pl.semaphore_wait(bar, 22)
 
     def ring_w(r):
         src = at4(x, -r)
-        if r:
+        if r == 2:
+            for d in range(2):
+                half = wbuf.at[z, k, src, pl.ds(d * 512, 512)]
+                arrived(half, xf_ss.at[1, d], xf_rs.at[1, d])
+        elif r:
             arrived(wbuf.at[z, k, src], x_ss.at[1, r], x_rs.at[1, r])
         for d in range(2):
             go(wbuf.at[z, k, src], wbuf.at[z, k, src], g_ss.at[1, d, r], g_rs.at[1, d, r], z_dev[d])
@@ -139,64 +166,108 @@
 
     def ring_a(r):
         src = at4(x, -r)
-        if r:
+        if r == 2:
+            for d in range(2):
+                arrived(abuf.at[y, src, d], xf_ss.at[0, d], xf_rs.at[0, d])
+        elif r:
             arrived(abuf.at[y, src], x_ss.at[0, r], x_rs.at[0, r])
         for d in range(2):
             go(abuf.at[y, src], abuf.at[y, src], g_ss.at[0, d, r], g_rs.at[0, d, r], y_dev[d])
 
+    beside = [x_dev[1], x_dev[3]]
+
+    def near_w(n, _):
+        r = 2 * n - 1
+        to = at4(x, r)
+        arrange_w(to, wtb.at[n])
+        remote(wtb.at[n], wbuf.at[z, k, x], x_ss.at[1, r], x_rs.at[1, r], dev(to, y, z, k)).start()
+        return 0
+
+    def near_a(n, _):
+        r = 2 * n - 1
+        to = at4(x, r)
+        arrange_a(to, atb.at[n])
+        remote(atb.at[n], abuf.at[y, x], x_ss.at[0, r], x_rs.at[0, r], dev(to, y, z, k)).start()
+        return 0
+
+    def stage_w():
+        for d in range(2):
+            go(wtb.at[0, pl.ds(d * 512, 512)], rw.at[d], x_ss.at[1, 2 * d], x_rs.at[1, 2 * d], beside[d])
+
+    def stage_a():
+        for d in range(2):
+            go(atb.at[0, d], ra.at[d], x_ss.at[0, 2 * d], x_rs.at[0, 2 * d], beside[d])
+
+    def relay_w():
+        for d in range(2):
+            arrived(rw.at[d], x_ss.at[1, 2 * d], x_rs.at[1, 2 * d])
+            go(rw.at[d], wbuf.at[z, k, at4(x, 2 * d - 1), pl.ds(d * 512, 512)], xf_ss.at[1, d], xf_rs.at[1, d], beside[d])
+
+    def relay_a():
+        for d in range(2):
+            arrived(ra.at[d], x_ss.at[0, 2 * d], x_rs.at[0, 2 * d])
+            go(ra.at[d], abuf.at[y, at4(x, 2 * d - 1), d], xf_ss.at[0, d], xf_rs.at[0, d], beside[d])
+
+    def forward_w(r):
+        src = at4(x, -r)
+        for d in range(2):
+            zz = at4(z, 2 * d - 1)
+            arrived(wbuf.at[zz, k, src], g_ss.at[1, d, r], g_rs.at[1, d, r])
+            half = wbuf.at[zz, k, src, pl.ds(d * 512, 512)]
+            go(half, half, f_ss.at[1, d, r], f_rs.at[1, d, r], z_dev[d])
+            go(wbuf.at[zz, k, src], wbuf.at[zz, k, src], s_ss.at[1 + d, r], s_rs.at[1 + d, r], sib)
+
+    def forward_a(r):
+        src = at4(x, -r)
+        for d in range(2):
+            yy = at4(y, 2 * d - 1)
+            arrived(abuf.at[yy, src], g_ss.at[0, d, r], g_rs.at[0, d, r])
+            go(abuf.at[yy, src, d], abuf.at[yy, src, d], f_ss.at[0, d, r], f_rs.at[0, d, r], y_dev[d])
+
+    def finish_w(r):
+        for d in range(2):
+            half = wbuf.at[at4(z, 2), k, at4(x, -r), pl.ds(d * 512, 512)]
+            arrived(half, f_ss.at[1, d, r], f_rs.at[1, d, r])
+            go(half, half, sf_ss.at[d, r], sf_rs.at[d, r], sib)
+
+    def finish_a(r):
+        for d in range(2):
+            arrived(abuf.at[at4(y, 2), at4(x, -r), d], f_ss.at[0, d, r], f_rs.at[0, d, r])
+
     ring_w(0)
+    lax.fori_loop(1, 3, near_w, 0)
     load_a.wait()
     for h, wide in enumerate((wide0, wide1)):
         wide[...] = av[:, :, h * LANES:(h + 1) * LANES].astype(F32).reshape(BA * BB, LANES)
     arrange_a(x, abuf.at[y, x])
     ring_a(0)
-
-    def share_out(n, _):
-        r = (1 + 2 * n) - 3 * (n // 2)
-        to = at4(x, r)
-        there = dev(to, y, z, k)
-        arrange_w(to, wtb.at[n])
-        remote(wtb.at[n], wbuf.at[z, k, x], x_ss.at[1, r], x_rs.at[1, r], there).start()
-        arrange_a(to, atb.at[n])
-        remote(atb.at[n], abuf.at[y, x], x_ss.at[0, r], x_rs.at[0, r], there).start()
-        return 0
-
-    lax.fori_loop(0, 3, share_out, 0)
-
-    def forward(r):
-        src = at4(x, -r)
-        for d in range(2):
-            yy, zz = at4(y, 2 * d - 1), at4(z, 2 * d - 1)
-            arrived(wbuf.at[zz, k, src], g_ss.at[1, d, r], g_rs.at[1, d, r])
-            half = wbuf.at[zz, k, src, pl.ds(d * 512, 512)]
-            go(half, half, f_ss.at[1, d, r], f_rs.at[1, d, r], z_dev[d])
-            go(wbuf.at[zz, k, src], wbuf.at[zz, k, src], s_ss.at[1 + d, r], s_rs.at[1 + d, r], sib)
-            arrived(abuf.at[yy, src], g_ss.at[0, d, r], g_rs.at[0, d, r])
-            go(abuf.at[yy, src, d], abuf.at[yy, src, d], f_ss.at[0, d, r], f_rs.at[0, d, r], y_dev[d])
-
-    def finish(r):
-        src = at4(x, -r)
-        yy, zz = at4(y, 2), at4(z, 2)
-        for d in range(2):
-            half = wbuf.at[zz, k, src, pl.ds(d * 512, 512)]
-            arrived(half, f_ss.at[1, d, r], f_rs.at[1, d, r])
-            go(half, half, sf_ss.at[d, r], sf_rs.at[d, r], sib)
-            arrived(abuf.at[yy, src, d], f_ss.at[0, d, r], f_rs.at[0, d, r])
-
-    forward(0)
+    lax.fori_loop(1, 3, near_a, 0)
+    arrange_w(at4(x, 2), wtb.at[0])
+    arrange_a(at4(x, 2), atb.at[0])
+    forward_w(0)
     ring_w(1)
+    ring_w(3)
+    stage_w()
+    forward_a(0)
     ring_a(1)
-    ring_w(3)
     ring_a(3)
-    finish(0)
-    forward(1)
+    stage_a()
+    forward_w(1)
+    relay_w()
+    forward_a(1)
+    relay_a()
     ring_w(2)
+    forward_w(3)
     ring_a(2)
-    forward(3)
-    finish(1)
-    forward(2)
-    finish(3)
-    finish(2)
+    forward_a(3)
+    finish_w(0)
+    finish_w(1)
+    forward_w(2)
+    finish_w(3)
+    forward_a(2)
+    finish_w(2)
+    for r in (0, 1, 3, 2):
+        finish_a(r)
     for r in range(4):
         src = at4(x, -r)
         arrived(wbuf.at[z, 1 - k, src], s_ss.at[0, r], s_rs.at[0, r])
@@ -209,7 +280,7 @@
 
     def quadrant(n, _):
         h, s = n // 4, lax.rem(n, 4)
-        to = lax.rem(x + s + 1, 4)
+        to = lax.rem(x + 2 - s + 3 * (s // 2) + 2 * (s // 3), 4)
         th, tl = to // 2, lax.rem(to, 2)
         split = [(hi, mid, lo) for hi in range(4) for mid in range(2) for lo in range(2)]
 
@@ -222,6 +293,7 @@
             return 0
 
         lax.fori_loop(0, 2, columns, 0)
+        tiles = []
         for t, (i, jj) in enumerate(TILES):
             ii, ip = i // 2, i % 2
             here = cbuf[i * 16:(i + 1) * 16, jj * LANES:(jj + 1) * LANES]
@@ -231,70 +303,159 @@
                 other = jnp.where(left, even, pltpu.roll(odd, BB, 1))
             else:
                 other = jnp.where(left, pltpu.roll(even, BB, 1), odd)
-            tile = here - other
-            dsum[pl.ds(h * (NT * 16) + t * 16, 16), :] = tile
-            dsend[n, t * 16:(t + 1) * 16, :] = tile.astype(BF16)
-
-        @pl.when(s < 3)
-        def _():
-            remote(dsend.at[n], drecv.at[n], d_ss.at[n], d_rs.at[n], dev(to, y, z, k)).start()
+            tiles.append(here - other)
+            if t % 2 == 0:
+                continue
+            for u in range(2):
+                pair = jnp.concatenate([v[u * 8:u * 8 + 8] for v in tiles], axis=0)
+                dsum[pl.ds((2 * h + u) * ROWS + (t - 1) * 8, 16), :] = pair
+                dsend[n, u, (t - 1) * 8:(t + 1) * 8, :] = pair.astype(BF16)
+            tiles = []
+
+        @pl.when(s == 0)
+        def _():
+            stage_d(2 * h)
+
+        @pl.when(lax.rem(s, 3) > 0)
+        def _():
+            near_d(2 * h, s)
+
+        @pl.when(s == 3)
+        def _():
+            relay_d(2 * h)
+            stage_d(2 * h + 1)
+            near_d(2 * h + 1, 1)
+            near_d(2 * h + 1, 2)
+
+        @pl.when(n == 5)
+        def _():
+            relay_d(1)
         return 0
 
+    def term(c, s):
+        return dsend.at[4 * (c // 2) + s, lax.rem(c, 2)]
+
+    def d_copy(c, e, src, dst, to):
+        return remote(src, dst, d_ss.at[c, e], d_rs.at[c, e], to)
+
+    def stage_copy(c, d):
+        return d_copy(c, d, term(c, 0).at[pl.ds(d * ROWS // 2, ROWS // 2)], rd.at[c, d], beside[d])
+
+    def near_copy(c, s):
+        return d_copy(c, s + 1, term(c, s), drecv.at[c, s], dev(at4(x, 3 - 2 * (2 - s)), y, z, k))
+
+    def relay_copy(c, d):
+        return d_copy(c, 4 + d, rd.at[c, d], drecv.at[c, 0, pl.ds(d * ROWS // 2, ROWS // 2)], beside[d])
+
+    def stage_d(c):
+        for d in range(2):
+            stage_copy(c, d).start()
+
+    def near_d(c, s):
+        near_copy(c, s).start()
+
+    def relay_d(c):
+        for d in range(2):
+            stage_copy(c, d).wait_recv()
+            relay_copy(c, d).start()
+
     lax.fori_loop(0, 8, quadrant, 0)
+    relay_d(3)
 
     left2 = lax.broadcasted_iota(jnp.int32, (BB, LANES), 1) < BB
-    b_mine = pl.ds(pl.multiple_of(k * BA, BA), BA)
-    b_other = pl.ds(pl.multiple_of((1 - k) * BA, BA), BA)
-    for h in range(2):
-        for s in range(3):
-            arrived(drecv.at[4 * h + s], d_ss.at[4 * h + s], d_rs.at[4 * h + s])
-        part = pl.ds(h * NT * 16, NT * 16)
-        dsum[part, :] = (dsum[part, :] + drecv[4 * h].astype(F32) + drecv[4 * h + 1].astype(F32)
-                         + drecv[4 * h + 2].astype(F32))
+
+    def block(q, c):
+        return xb.at[(k, 1 - k)[q], pl.ds(c * 8, 8)]
+
+    def direct(q, c):
+        return remote(block(q, c), ybuf.at[k, pl.ds(c * 8, 8)], m_ss.at[q, c], m_rs.at[q, c], m_dev[q])
+
+    def same_chip(c):
+        return pltpu.make_async_copy(block(0, c), ybuf.at[k, pl.ds(c * 8, 8)], l_sem.at[2 + c])
+
+    def to_corner(q, c):
+        if q == 0:
+            corner, slot = dev(turned, z, z, k), lax.rem(y - z + 3, 4)
+        else:
+            corner, slot = dev(turned, y, y, 1 - k), lax.rem(z - y + 3, 4)
+        return remote(block(q, c), mid.at[q, c, slot], e_ss.at[q, c], e_rs.at[q, c, slot], corner)
+
+    def from_corner(q, c, j):
+        there = dev(x, y, at4(z, 1 + j), k) if q == 0 else dev(x, at4(y, 1 + j), z, k)
+        slot = k if q == 0 else 1 - k
+        return remote(mid.at[q, c, j], ybuf.at[slot, pl.ds(c * 8, 8)], p_ss.at[q, c, j], m_rs.at[q, c], there)
+
+    def pass_on(c):
+        @pl.when(diagonal)
+        def _():
+            for q in range(2):
+                def one(j, _):
+                    arrived(mid.at[q, c, j], e_ss.at[q, c], e_rs.at[q, c, j])
+                    from_corner(q, c, j).start()
+                    return 0
+
+                lax.fori_loop(0, 3, one, 0)
+
+    for c in range(4):
+        for s in (1, 2):
+            near_copy(c, s).wait_recv()
+        for d in range(2):
+            relay_copy(c, d).wait_recv()
+        part = pl.ds(c * ROWS, ROWS)
+        dsum[part, :] = dsum[part, :] + drecv[c, 0].astype(F32) + drecv[c, 1].astype(F32) + drecv[c, 2].astype(F32)
 
         def turn(p, _):
             rows = jnp.concatenate(
-                [dsum[pl.ds(h * NT * 16 + 2 * p + q, NT, stride=16), :] for q in range(2)], axis=0)
+                [dsum[pl.ds(c * ROWS + 2 * p + q, NT, stride=8), :] for q in range(2)], axis=0)
             t = rows.T
             lo, hi = t[:BB], t[BB:]
             first = jnp.where(left2, lo, pltpu.roll(hi, BB, 1))
             second = jnp.where(left2, pltpu.roll(lo, BB, 1), hi)
-            at = h * 16 + 2 * p
+            at = c * 8 + 2 * p
             xf[at] = first
             xf[at + 1] = second
-            xb[at] = first.astype(BF16)
-            xb[at + 1] = second.astype(BF16)
+            xb[0, at] = first[:BA].astype(BF16)
+            xb[1, at] = first[BA:].astype(BF16)
+            xb[0, at + 1] = second[:BA].astype(BF16)
+            xb[1, at + 1] = second[BA:].astype(BF16)
             return 0
 
-        lax.fori_loop(0, 8, turn, 0)
-        a_part = pl.ds(h * 16, 16)
-        go(xb.at[a_part, b_other], ybuf.at[k, a_part], m_ss.at[1, h], m_rs.at[1, h], m_dev[1])
-        same = (xb.at[a_part, b_mine], ybuf.at[k, a_part])
-
+        lax.fori_loop(0, 4, turn, 0)
+
+        @pl.when(jnp.logical_not(diagonal))
+        def _():
+            to_corner(0, c).start()
+            to_corner(1, c).start()
+
+        @pl.when(diagonal)
+        def _():
+            direct(1, c).start()
+
+            @pl.when(own_turned)
+            def _():
+                same_chip(c).start()
+
+            @pl.when(jnp.logical_not(own_turned))
+            def _():
+                direct(0, c).start()
+
+        if c:
+            pass_on(c - 1)
+    pass_on(3)
+
+    for c in range(4):
         @pl.when(own_turned)
         def _():
-            pltpu.make_async_copy(*same, l_sem.at[2 + h]).start()
+            same_chip(c).wait()
 
         @pl.when(jnp.logical_not(own_turned))
         def _():
-            remote(*same, m_ss.at[0, h], m_rs.at[0, h], m_dev[0]).start()
-
-    for h in range(2):
-        a_part = pl.ds(h * 16, 16)
-        same = (xb.at[a_part, b_mine], ybuf.at[k, a_part])
-
-        @pl.when(own_turned)
-        def _():
-            pltpu.make_async_copy(*same, l_sem.at[2 + h]).wait()
-
-        @pl.when(jnp.logical_not(own_turned))
-        def _():
-            remote(*same, m_ss.at[0, h], m_rs.at[0, h], m_dev[0]).wait()
-
-        arrived(ybuf.at[1 - k, a_part], m_ss.at[1, h], m_rs.at[1, h])
-        for c in range(2):
-            at = c * BA * BA + h * 16 * BA
-            yf[at:at + 16 * BA, :] = ybuf[c, h * 16:h * 16 + 16].astype(F32).reshape(16 * BA, LANES)
+            arrived(ybuf.at[k, pl.ds(c * 8, 8)], m_ss.at[0, c], m_rs.at[0, c])
+
+        arrived(ybuf.at[1 - k, pl.ds(c * 8, 8)], m_ss.at[1, c], m_rs.at[1, c])
+        for v in range(2):
+            at = v * BA * BA + c * 8 * BA
+            yf[at:at + 8 * BA, :] = ybuf[v, c * 8:c * 8 + 8].astype(F32).reshape(8 * BA, LANES)
 
     def mirror(a, _):
         r_ref[a] = xf[a] - yf[pl.ds(a, BB, stride=BA), :]
@@ -303,13 +464,31 @@
     lax.fori_loop(0, BA, mirror, 0)
     for copy in sends:
         copy.wait_send()
-    for n, r in enumerate((1, 3, 2)):
+    for n, r in ((1, 1), (2, 3)):
         remote(wtb.at[n], wbuf.at[z, k, x], x_ss.at[1, r], x_rs.at[1, r], sib).wait_send()
         remote(atb.at[n], abuf.at[y, x], x_ss.at[0, r], x_rs.at[0, r], sib).wait_send()
-    for h in range(2):
-        for s in range(3):
-            n = 4 * h + s
-            remote(dsend.at[n], drecv.at[n], d_ss.at[n], d_rs.at[n], sib).wait_send()
+    for c in range(4):
+        for s in (1, 2):
+            near_copy(c, s).wait_send()
+        for d in range(2):
+            stage_copy(c, d).wait_send()
+            relay_copy(c, d).wait_send()
+
+        @pl.when(jnp.logical_not(diagonal))
+        def _():
+            to_corner(0, c).wait_send()
+            to_corner(1, c).wait_send()
+
+        @pl.when(diagonal)
+        def _():
+            direct(1, c).wait_send()
+            for q in range(2):
+                for j in range(3):
+                    from_corner(q, c, j).wait_send()
+
+            @pl.when(jnp.logical_not(own_turned))
+            def _():
+                direct(0, c).wait_send()
 
 
 STEP = 8
@@ -338,18 +517,23 @@
             pltpu.VMEM((BA * BB, LANES), F32),
             pltpu.VMEM((3, 2, 512, LANES), BF16),
             pltpu.VMEM((3, 1024, LANES), BF16),
+            pltpu.VMEM((2, 512, LANES), BF16),
+            pltpu.VMEM((2, 512, LANES), BF16),
+            pltpu.VMEM((4, 2, ROWS // 2, LANES), BF16),
             pltpu.VMEM((4, 4, 2, 512, LANES), BF16),
             pltpu.VMEM((4, 2, 4, 1024, LANES), BF16),
             pltpu.VMEM((256, 1024), F32),
-            pltpu.VMEM((8, NT * 16, LANES), BF16),
-            pltpu.VMEM((8, NT * 16, LANES), BF16),
+            pltpu.VMEM((8, 2, ROWS, LANES), BF16),
+            pltpu.VMEM((4, 3, ROWS, LANES), BF16),
             pltpu.VMEM((NT * BA, LANES), F32),
             pltpu.VMEM((BA, BB, LANES), F32),
-            pltpu.VMEM((BA, BB, LANES), BF16),
+            pltpu.VMEM((2, BA, BA, LANES), BF16),
+            pltpu.VMEM((2, 4, 3, 8, BA, LANES), BF16),
             pltpu.VMEM((2, BA, BA, LANES), BF16),
             pltpu.VMEM((2 * BA * BA, LANES), F32),
-            dma((2, 4)), dma((2, 4)), dma((2, 2, 4)), dma((2, 2, 4)), dma((2, 2, 4)), dma((2, 2, 4)),
-            dma((3, 4)), dma((3, 4)), dma((2, 4)), dma((2, 4)), dma((8,)), dma((8,)), dma((2, 2)), dma((2, 2)), dma((4,)),
+            dma((2, 4)), dma((2, 4)), dma((2, 2)), dma((2, 2)), dma((2, 2, 4)), dma((2, 2, 4)), dma((2, 2, 4)), dma((2, 2, 4)),
+            dma((3, 4)), dma((3, 4)), dma((2, 4)), dma((2, 4)), dma((4, 6)), dma((4, 6)),
+            dma((2, 4)), dma((2, 4, 3)), dma((2, 4, 3)), dma((2, 4)), dma((2, 4)), dma((6,)),
         ],
         compiler_params=pltpu.CompilerParams(collective_id=0, has_side_effects=True, vmem_limit_bytes=48 << 20),
         name="cycle",

time: 113 us -> 103 us (0.912); the launches traced: 113 us -> 101 us
  Pallas kernels: 109 us -> 97 us
    pallas_call x1, Pallas kernels: 106 us -> 94.6 us  [local(): pl.pallas_call(cycle_kernel, out_shape=jax.ShapeDtypeStruct((BA, BB, LANE...]
where the time goes in v3:
time: 103 us; the launch traced here: 101 us
  Pallas kernels  97 us (94%)
  local copies, waits for them, and re-layouts  3.55 us (3%)
    pallas_call x1, Pallas kernels, local(): pl.pallas_call(cycle_kernel, out_shape=jax.ShapeDtypeStruct((BA, BB, LANE...  94.6 us
    unnamed x8, local copies, waits for them, and re-layouts  3.14 us
    pallas_call x1, Pallas kernels, local(): pl.pallas_call(update_kernel, grid=(BA // STEP,), out_shape=jax.ShapeDtyp...  2.36 us

profile of v3, /device:TPU:11, one launch (start us, length us, event | category | flops | bytes accessed | tf_op | source)
XLA Modules:
  0.0 101.4 jit_solution(14411296516309336958)
XLA Ops:
  0.0 0.0 copy-start
  0.0 0.7 copy-done
  0.7 0.1 dynamic-slice_bitcast_fusion
  0.8 0.1 dynamic-slice_bitcast_fusion.1
  0.8 0.8 broadcast_add_fusion
  1.6 0.1 add.32.occ_ref
  1.7 0.1 copy.6.vrow_ref
  1.8 0.1 copy.7.vcol_ref
  1.9 0.0 copy-start.1
  1.9 1.2 %copy-done.1 = bf16[32,64,256]{2,1,0:T(8,128)(2,1)S(1)} copy-done((bf16[32,64,256]{2,1,0:T(8,128)(2,1)S(1)}, bf16[32,64,256]{2,1,0:T(8,128)(2,1)}, u32[]{:S(2)}) %copy-start.1) | copy-done | bytes 1048600
  3.1 0.0 copy-start.2
  3.1 1.2 %copy-done.2 = bf16[32,64,256]{2,1,0:T(8,128)(2,1)S(1)} copy-done((bf16[32,64,256]{2,1,0:T(8,128)(2,1)S(1)}, bf16[32,64,256]{2,1,0:T(8,128)(2,1)}, u32[]{:S(2)}) %copy-start.2) | copy-done | bytes 1048600
  4.4 0.0 copy-start.3
  4.4 94.6 %cycle.1.r_ref = f32[32,64,128]{2,1,0:T(8,128)S(1)} custom-call(bf16[32,64,256]{2,1,0:T(8,128)(2,1)S(1)} %copy-done.1, bf16[32,64,256]{2,1,0:T(8,128)(2,1)S(1)} %copy-done.2), custom_call_target="tpu_custom_call" | custom-call | tf_op jit(solution)/shard_map/cycle/pallas_call | solution.py:508
  99.0 0.0 copy-done.3
  99.0 2.4 %update.1 = f32[32,64,256]{2,1,0:T(8,128)} custom-call(bf16[32,64,256]{2,1,0:T(8,128)(2,1)S(1)} %copy-done.1, f32[32,64,128]{2,1,0:T(8,128)S(1)} %cycle.1.r_ref, bf16[256,256]{1,0:T(8,128)(2,1)S(1)} %copy-done.3, f32[1,256]{1,0:T(1,128)S(1)} %add.32.occ_ref, f32[32,1,1]{2,1,0:T(1,128)S(1)} %copy.6.vrow_ref, f32[64,1]{1,0:T(8,128)S(1)} %copy.7.vcol_ref), custom_call_target="tpu_custom_call" | custom-call | tf_op jit(solution)/shard_map/update/pallas_call | solution.py:546
Async XLA Ops:
  0.0 0.7 copy-start
  1.9 1.2 %copy-start.1 = (bf16[32,64,256]{2,1,0:T(8,128)(2,1)S(1)}, bf16[32,64,256]{2,1,0:T(8,128)(2,1)}, u32[]{:S(2)}) copy-start(bf16[32,64,256]{2,1,0:T(8,128)(2,1)} %a_ref.1) | copy-start | bytes 3145732
  3.1 1.2 %copy-start.2 = (bf16[32,64,256]{2,1,0:T(8,128)(2,1)S(1)}, bf16[32,64,256]{2,1,0:T(8,128)(2,1)}, u32[]{:S(2)}) copy-start(bf16[32,64,256]{2,1,0:T(8,128)(2,1)} %w_hbm.1) | copy-start | bytes 3145732
  4.4 94.6 %copy-start.3 = (bf16[256,256]{1,0:T(8,128)(2,1)S(1)}, bf16[256,256]{1,0:T(8,128)(2,1)}, u32[]{:S(2)}) copy-start(bf16[256,256]{1,0:T(8,128)(2,1)} %constant.19.clone.sel_ref) | copy-start | bytes 393220

commit v4 on v3

--- a/solution.py
+++ b/solution.py
@@ -19,6 +19,7 @@
 ANY = pl.BlockSpec(memory_space=pl.ANY)
 TILES = [(i, jj) for i in range(OCC) for jj in range((i + 1) // 2, OCC // 2)]
 NT = len(TILES)
+STRAIGHT = {(0, 0), (0, 1), (0, 2), (0, 3), (1, 3)}
 ROWS = NT * 8
 
 
@@ -92,7 +93,7 @@
 
     @pl.when(jnp.logical_not(diagonal))
     def _():
-        for d in (dev(turned, z, z, k), dev(turned, y, y, 1 - k), dev(x, y, y, k), dev(x, z, z, k)):
+        for d in (dev(turned, z, z, k), dev(turned, y, y, 1 - k), dev(x, y, y, k), dev(x, z, z, k), m_dev[0], m_dev[1]):
             greet(d)
 
     load_a = pltpu.make_async_copy(a_hbm, av, l_sem.at[0])
@@ -142,7 +143,7 @@
 
     @pl.when(jnp.logical_not(diagonal))
     def _():
-        pl.semaphore_wait(bar, 12)
+        pl.semaphore_wait(bar, 14)
 
     @pl.when(own_turned)
     def _():
@@ -330,6 +331,10 @@
         @pl.when(n == 5)
         def _():
             relay_d(1)
+
+        @pl.when(n == 6)
+        def _():
+            settle(0)
         return 0
 
     def term(c, s):
@@ -359,8 +364,6 @@
             stage_copy(c, d).wait_recv()
             relay_copy(c, d).start()
 
-    lax.fori_loop(0, 8, quadrant, 0)
-    relay_d(3)
 
     left2 = lax.broadcasted_iota(jnp.int32, (BB, LANES), 1) < BB
 
@@ -389,6 +392,9 @@
         @pl.when(diagonal)
         def _():
             for q in range(2):
+                if (q, c) in STRAIGHT:
+                    continue
+
                 def one(j, _):
                     arrived(mid.at[q, c, j], e_ss.at[q, c], e_rs.at[q, c, j])
                     from_corner(q, c, j).start()
@@ -396,7 +402,7 @@
 
                 lax.fori_loop(0, 3, one, 0)
 
-    for c in range(4):
+    def settle(c):
         for s in (1, 2):
             near_copy(c, s).wait_recv()
         for d in range(2):
@@ -424,8 +430,8 @@
 
         @pl.when(jnp.logical_not(diagonal))
         def _():
-            to_corner(0, c).start()
-            to_corner(1, c).start()
+            for q in range(2):
+                (direct if (q, c) in STRAIGHT else to_corner)(q, c).start()
 
         @pl.when(diagonal)
         def _():
@@ -439,8 +445,12 @@
             def _():
                 direct(0, c).start()
 
-        if c:
-            pass_on(c - 1)
+
+    lax.fori_loop(0, 8, quadrant, 0)
+    relay_d(3)
+    for c in range(1, 4):
+        settle(c)
+        pass_on(c - 1)
     pass_on(3)
 
     for c in range(4):
@@ -476,15 +486,16 @@
 
         @pl.when(jnp.logical_not(diagonal))
         def _():
-            to_corner(0, c).wait_send()
-            to_corner(1, c).wait_send()
+            for q in range(2):
+                (direct if (q, c) in STRAIGHT else to_corner)(q, c).wait_send()
 
         @pl.when(diagonal)
         def _():
             direct(1, c).wait_send()
             for q in range(2):
-                for j in range(3):
-                    from_corner(q, c, j).wait_send()
+                if (q, c) not in STRAIGHT:
+                    for j in range(3):
+                        from_corner(q, c, j).wait_send()
 
             @pl.when(jnp.logical_not(own_turned))
             def _():
@@ -499,7 +510,12 @@
     hi = r.astype(BF16)
     lo = (r - hi.astype(F32)).astype(BF16)
     full = jnp.dot(jnp.concatenate([hi, lo], axis=1), sel_ref[...], preferred_element_type=F32)
-    den = (occ_ref[...][None] - vrow_ref[...]) - vcol_ref[...][None]
+    lane = lax.broadcasted_iota(jnp.int32, (1, PAIRS), 1)
+    occ_i, occ_j = jnp.zeros((1, PAIRS), F32), jnp.zeros((1, PAIRS), F32)
+    for n in range(OCC):
+        occ_i = jnp.where((lane >> 4) == n, occ_ref[n], occ_i)
+        occ_j = jnp.where((lane & 15) == n, occ_ref[n], occ_j)
+    den = ((occ_i + occ_j)[None] - vrow_ref[...]) - vcol_ref[...][None]
     o_ref[...] = a_ref[...].astype(F32) + full.reshape(STEP, BB, PAIRS) / den
 
 
@@ -541,7 +557,6 @@
     row_pos, col_pos = lax.axis_index("row"), lax.axis_index("col")
     vir_rows = lax.dynamic_slice_in_dim(vir_energy, row_pos * BA, BA).reshape(BA, 1, 1)
     vir_cols = lax.dynamic_slice_in_dim(vir_energy, col_pos * BB, BB).reshape(BB, 1)
-    occ = (occ_energy[:, None] + occ_energy[None, :]).reshape(1, PAIRS)
     sel = jnp.asarray(spread_matrix(), BF16)
     return pl.pallas_call(
         update_kernel,
@@ -551,14 +566,14 @@
             pl.BlockSpec((STEP, BB, PAIRS), lambda s: (s, 0, 0)),
             pl.BlockSpec((STEP, BB, LANES), lambda s: (s, 0, 0)),
             pl.BlockSpec((2 * LANES, PAIRS), lambda s: (0, 0)),
-            pl.BlockSpec((1, PAIRS), lambda s: (0, 0)),
+            pl.BlockSpec(memory_space=pltpu.SMEM),
             pl.BlockSpec((STEP, 1, 1), lambda s: (s, 0, 0)),
             pl.BlockSpec((BB, 1), lambda s: (0, 0)),
         ],
         out_specs=pl.BlockSpec((STEP, BB, PAIRS), lambda s: (s, 0, 0)),
         compiler_params=pltpu.CompilerParams(vmem_limit_bytes=40 << 20),
         name="update",
-    )(amplitudes, resid, sel, occ, vir_rows, vir_cols)
+    )(amplitudes, resid, sel, occ_energy, vir_rows, vir_cols)
 
 
 def solution(mesh):

time: 103 us -> 99.3 us (0.964); the launches traced: 101 us -> 98.8 us
  Pallas kernels: 97 us -> 95.3 us
    pallas_call x1, Pallas kernels: 94.6 us -> 92.4 us  [local(): pl.pallas_call(cycle_kernel, out_shape=jax.ShapeDtypeStruct((BA, BB, LANE...]
    unnamed x8 -> x10, local copies, waits for them, and re-layouts: 3.14 us -> 3.14 us
where the time goes in v4:
time: 99.3 us; the launch traced here: 98.8 us
  Pallas kernels  95.3 us (96%)
  local copies, waits for them, and re-layouts  3.47 us (3%)
    pallas_call x1, Pallas kernels, local(): pl.pallas_call(cycle_kernel, out_shape=jax.ShapeDtypeStruct((BA, BB, LANE...  92.4 us
    unnamed x10, local copies, waits for them, and re-layouts  3.14 us
    pallas_call x1, Pallas kernels, local(): pl.pallas_call(update_kernel, grid=(BA // STEP,), out_shape=jax.ShapeDtyp...  2.92 us

profile of v4, /device:TPU:11, one launch (start us, length us, event | category | flops | bytes accessed | tf_op | source)
XLA Modules:
  0.0 98.8 jit_solution(7589411544457554060)
XLA Ops:
  0.0 0.0 copy-start
  0.0 0.0 copy-start.4
  0.0 0.7 copy-done
  0.7 0.1 dynamic-slice_bitcast_fusion
  0.8 0.1 dynamic-slice_bitcast_fusion.1
  0.8 0.1 copy.6.vrow_ref
  0.9 0.1 copy.7.vcol_ref
  1.0 0.0 copy-start.1
  1.0 1.2 %copy-done.1 = bf16[32,64,256]{2,1,0:T(8,128)(2,1)S(1)} copy-done((bf16[32,64,256]{2,1,0:T(8,128)(2,1)S(1)}, bf16[32,64,256]{2,1,0:T(8,128)(2,1)}, u32[]{:S(2)}) %copy-start.1) | copy-done | bytes 1048600
  2.2 0.0 copy-start.2
  2.2 1.2 %copy-done.2 = bf16[32,64,256]{2,1,0:T(8,128)(2,1)S(1)} copy-done((bf16[32,64,256]{2,1,0:T(8,128)(2,1)S(1)}, bf16[32,64,256]{2,1,0:T(8,128)(2,1)}, u32[]{:S(2)}) %copy-start.2) | copy-done | bytes 1048600
  3.5 0.0 copy-start.3
  3.5 92.4 %cycle.1.r_ref = f32[32,64,128]{2,1,0:T(8,128)S(1)} custom-call(bf16[32,64,256]{2,1,0:T(8,128)(2,1)S(1)} %copy-done.1, bf16[32,64,256]{2,1,0:T(8,128)(2,1)S(1)} %copy-done.2), custom_call_target="tpu_custom_call" | custom-call | tf_op jit(solution)/shard_map/cycle/pallas_call | solution.py:524
  95.8 0.0 copy-done.4
  95.8 0.0 copy-done.3
  95.9 2.9 %update.1 = f32[32,64,256]{2,1,0:T(8,128)} custom-call(bf16[32,64,256]{2,1,0:T(8,128)(2,1)S(1)} %copy-done.1, f32[32,64,128]{2,1,0:T(8,128)S(1)} %cycle.1.r_ref, bf16[256,256]{1,0:T(8,128)(2,1)S(1)} %copy-done.3, f32[16]{0:T(128)S(1)} %copy-done.4, f32[32,1,1]{2,1,0:T(1,128)S(1)} %copy.6.vrow_ref, f32[64,1]{1,0:T(8,128)S(1)} %copy.7.vcol_ref), custom_call_target="tpu_custom_call" | custom-call | tf_op jit(solution)/shard_map/update/pallas_call | solution.py:561
Async XLA Ops:
  0.0 0.7 copy-start
  0.0 95.8 %copy-start.4 = (f32[16]{0:T(128)S(1)}, f32[16]{0:T(128)}, u32[]{:S(2)}) copy-start(f32[16]{0:T(128)} %occ_ref.1) | copy-start | bytes 196
  1.0 1.2 %copy-start.1 = (bf16[32,64,256]{2,1,0:T(8,128)(2,1)S(1)}, bf16[32,64,256]{2,1,0:T(8,128)(2,1)}, u32[]{:S(2)}) copy-start(bf16[32,64,256]{2,1,0:T(8,128)(2,1)} %a_ref.1) | copy-start | bytes 3145732
  2.2 1.2 %copy-start.2 = (bf16[32,64,256]{2,1,0:T(8,128)(2,1)S(1)}, bf16[32,64,256]{2,1,0:T(8,128)(2,1)}, u32[]{:S(2)}) copy-start(bf16[32,64,256]{2,1,0:T(8,128)(2,1)} %w_hbm.1) | copy-start | bytes 3145732
  3.5 92.4 %copy-start.3 = (bf16[256,256]{1,0:T(8,128)(2,1)S(1)}, bf16[256,256]{1,0:T(8,128)(2,1)}, u32[]{:S(2)}) copy-start(bf16[256,256]{1,0:T(8,128)(2,1)} %constant.19.clone.sel_ref) | copy-start | bytes 393220

commit v5 on v4

--- a/solution.py
+++ b/solution.py
@@ -288,12 +288,12 @@
         def columns(n, _):
             rows = pl.ds(pl.multiple_of(h * 256, 256), 256)
             lhs = jnp.concatenate([abuf[hi, 2 * th + mid, lo, rows] for hi, mid, lo in split], axis=1)
-            rhs = jnp.concatenate([wbuf[hi, lo, 2 * mid + tl, pl.ds(n * 512, 512)] for hi, mid, lo in split], axis=1)
-            cbuf[:, pl.ds(pl.multiple_of(n * 512, 512), 512)] = lax.dot_general(
+            rhs = jnp.concatenate([wbuf[hi, lo, 2 * mid + tl, pl.ds(n, 1024)] for hi, mid, lo in split], axis=1)
+            cbuf[...] = lax.dot_general(
                 lhs, rhs, (((1,), (1,)), ((), ())), preferred_element_type=F32)
             return 0
 
-        lax.fori_loop(0, 2, columns, 0)
+        columns(0, 0)
         tiles = []
         for t, (i, jj) in enumerate(TILES):
             ii, ip = i // 2, i % 2

time: 99.3 us -> 97.9 us (0.986)
  Pallas kernels: 95.3 us -> 93.9 us
    pallas_call x1, Pallas kernels: 92.4 us -> 91 us  [local(): pl.pallas_call(cycle_kernel, out_shape=jax.ShapeDtypeStruct((BA, BB, LANE...]
where the time goes in v5:
time: 97.9 us; the launch traced here: 97.4 us
  Pallas kernels  93.9 us (96%)
  local copies, waits for them, and re-layouts  3.47 us (4%)
    pallas_call x1, Pallas kernels, local(): pl.pallas_call(cycle_kernel, out_shape=jax.ShapeDtypeStruct((BA, BB, LANE...  91 us
    unnamed x10, local copies, waits for them, and re-layouts  3.14 us
    pallas_call x1, Pallas kernels, local(): pl.pallas_call(update_kernel, grid=(BA // STEP,), out_shape=jax.ShapeDtyp...  2.91 us

profile of v5, /device:TPU:11, one launch (start us, length us, event | category | flops | bytes accessed | tf_op | source)
XLA Modules:
  0.0 97.4 jit_solution(12028065854544252108)
XLA Ops:
  0.0 0.0 copy-start
  0.0 0.0 copy-start.4
  0.0 0.7 copy-done
  0.7 0.1 dynamic-slice_bitcast_fusion
  0.8 0.1 dynamic-slice_bitcast_fusion.1
  0.8 0.1 copy.6.vrow_ref
  0.9 0.1 copy.7.vcol_ref
  1.0 0.0 copy-start.1
  1.0 1.2 %copy-done.1 = bf16[32,64,256]{2,1,0:T(8,128)(2,1)S(1)} copy-done((bf16[32,64,256]{2,1,0:T(8,128)(2,1)S(1)}, bf16[32,64,256]{2,1,0:T(8,128)(2,1)}, u32[]{:S(2)}) %copy-start.1) | copy-done | bytes 1048600
  2.2 0.0 copy-start.2
  2.2 1.2 %copy-done.2 = bf16[32,64,256]{2,1,0:T(8,128)(2,1)S(1)} copy-done((bf16[32,64,256]{2,1,0:T(8,128)(2,1)S(1)}, bf16[32,64,256]{2,1,0:T(8,128)(2,1)}, u32[]{:S(2)}) %copy-start.2) | copy-done | bytes 1048600
  3.5 0.0 copy-start.3
  3.5 91.0 %cycle.1.r_ref = f32[32,64,128]{2,1,0:T(8,128)S(1)} custom-call(bf16[32,64,256]{2,1,0:T(8,128)(2,1)S(1)} %copy-done.1, bf16[32,64,256]{2,1,0:T(8,128)(2,1)S(1)} %copy-done.2), custom_call_target="tpu_custom_call" | custom-call | tf_op jit(solution)/shard_map/cycle/pallas_call | solution.py:524
  94.4 0.0 copy-done.4
  94.4 0.0 copy-done.3
  94.5 2.9 %update.1 = f32[32,64,256]{2,1,0:T(8,128)} custom-call(bf16[32,64,256]{2,1,0:T(8,128)(2,1)S(1)} %copy-done.1, f32[32,64,128]{2,1,0:T(8,128)S(1)} %cycle.1.r_ref, bf16[256,256]{1,0:T(8,128)(2,1)S(1)} %copy-done.3, f32[16]{0:T(128)S(1)} %copy-done.4, f32[32,1,1]{2,1,0:T(1,128)S(1)} %copy.6.vrow_ref, f32[64,1]{1,0:T(8,128)S(1)} %copy.7.vcol_ref), custom_call_target="tpu_custom_call" | custom-call | tf_op jit(solution)/shard_map/update/pallas_call | solution.py:561
Async XLA Ops:
  0.0 0.7 copy-start
  0.0 94.4 %copy-start.4 = (f32[16]{0:T(128)S(1)}, f32[16]{0:T(128)}, u32[]{:S(2)}) copy-start(f32[16]{0:T(128)} %occ_ref.1) | copy-start | bytes 196
  1.0 1.2 %copy-start.1 = (bf16[32,64,256]{2,1,0:T(8,128)(2,1)S(1)}, bf16[32,64,256]{2,1,0:T(8,128)(2,1)}, u32[]{:S(2)}) copy-start(bf16[32,64,256]{2,1,0:T(8,128)(2,1)} %a_ref.1) | copy-start | bytes 3145732
  2.2 1.2 %copy-start.2 = (bf16[32,64,256]{2,1,0:T(8,128)(2,1)S(1)}, bf16[32,64,256]{2,1,0:T(8,128)(2,1)}, u32[]{:S(2)}) copy-start(bf16[32,64,256]{2,1,0:T(8,128)(2,1)} %w_hbm.1) | copy-start | bytes 3145732
  3.5 91.0 %copy-start.3 = (bf16[256,256]{1,0:T(8,128)(2,1)S(1)}, bf16[256,256]{1,0:T(8,128)(2,1)}, u32[]{:S(2)}) copy-start(bf16[256,256]{1,0:T(8,128)(2,1)} %constant.19.clone.sel_ref) | copy-start | bytes 393220

commit v6 on v5

--- a/solution.py
+++ b/solution.py
@@ -261,11 +261,11 @@
     forward_w(3)
     ring_a(2)
     forward_a(3)
+    forward_w(2)
+    forward_a(2)
     finish_w(0)
     finish_w(1)
-    forward_w(2)
     finish_w(3)
-    forward_a(2)
     finish_w(2)
     for r in (0, 1, 3, 2):
         finish_a(r)

time: 97.9 us -> 97.9 us (level)
  no operation moved by 1% of the time
where the time goes in v6:
time: 97.9 us; the launch traced here: 97.4 us
  Pallas kernels  93.9 us (96%)
  local copies, waits for them, and re-layouts  3.47 us (4%)
    pallas_call x1, Pallas kernels, local(): pl.pallas_call(cycle_kernel, out_shape=jax.ShapeDtypeStruct((BA, BB, LANE...  91 us
    unnamed x10, local copies, waits for them, and re-layouts  3.14 us
    pallas_call x1, Pallas kernels, local(): pl.pallas_call(update_kernel, grid=(BA // STEP,), out_shape=jax.ShapeDtyp...  2.92 us

profile of v6, /device:TPU:11, one launch (start us, length us, event | category | flops | bytes accessed | tf_op | source)
XLA Modules:
  0.0 97.4 jit_solution(1993360472611651307)
XLA Ops:
  0.0 0.0 copy-start
  0.0 0.0 copy-start.4
  0.0 0.7 copy-done
  0.7 0.1 dynamic-slice_bitcast_fusion
  0.8 0.1 dynamic-slice_bitcast_fusion.1
  0.8 0.1 copy.6.vrow_ref
  0.9 0.1 copy.7.vcol_ref
  1.0 0.0 copy-start.1
  1.0 1.2 %copy-done.1 = bf16[32,64,256]{2,1,0:T(8,128)(2,1)S(1)} copy-done((bf16[32,64,256]{2,1,0:T(8,128)(2,1)S(1)}, bf16[32,64,256]{2,1,0:T(8,128)(2,1)}, u32[]{:S(2)}) %copy-start.1) | copy-done | bytes 1048600
  2.2 0.0 copy-start.2
  2.2 1.2 %copy-done.2 = bf16[32,64,256]{2,1,0:T(8,128)(2,1)S(1)} copy-done((bf16[32,64,256]{2,1,0:T(8,128)(2,1)S(1)}, bf16[32,64,256]{2,1,0:T(8,128)(2,1)}, u32[]{:S(2)}) %copy-start.2) | copy-done | bytes 1048600
  3.5 0.0 copy-start.3
  3.5 91.0 %cycle.1.r_ref = f32[32,64,128]{2,1,0:T(8,128)S(1)} custom-call(bf16[32,64,256]{2,1,0:T(8,128)(2,1)S(1)} %copy-done.1, bf16[32,64,256]{2,1,0:T(8,128)(2,1)S(1)} %copy-done.2), custom_call_target="tpu_custom_call" | custom-call | tf_op jit(solution)/shard_map/cycle/pallas_call | solution.py:524
  94.5 0.0 copy-done.4
  94.5 0.0 copy-done.3
  94.5 2.9 %update.1 = f32[32,64,256]{2,1,0:T(8,128)} custom-call(bf16[32,64,256]{2,1,0:T(8,128)(2,1)S(1)} %copy-done.1, f32[32,64,128]{2,1,0:T(8,128)S(1)} %cycle.1.r_ref, bf16[256,256]{1,0:T(8,128)(2,1)S(1)} %copy-done.3, f32[16]{0:T(128)S(1)} %copy-done.4, f32[32,1,1]{2,1,0:T(1,128)S(1)} %copy.6.vrow_ref, f32[64,1]{1,0:T(8,128)S(1)} %copy.7.vcol_ref), custom_call_target="tpu_custom_call" | custom-call | tf_op jit(solution)/shard_map/update/pallas_call | solution.py:561
Async XLA Ops:
  0.0 0.7 copy-start
  0.0 94.5 %copy-start.4 = (f32[16]{0:T(128)S(1)}, f32[16]{0:T(128)}, u32[]{:S(2)}) copy-start(f32[16]{0:T(128)} %occ_ref.1) | copy-start | bytes 196
  1.0 1.2 %copy-start.1 = (bf16[32,64,256]{2,1,0:T(8,128)(2,1)S(1)}, bf16[32,64,256]{2,1,0:T(8,128)(2,1)}, u32[]{:S(2)}) copy-start(bf16[32,64,256]{2,1,0:T(8,128)(2,1)} %a_ref.1) | copy-start | bytes 3145732
  2.2 1.2 %copy-start.2 = (bf16[32,64,256]{2,1,0:T(8,128)(2,1)S(1)}, bf16[32,64,256]{2,1,0:T(8,128)(2,1)}, u32[]{:S(2)}) copy-start(bf16[32,64,256]{2,1,0:T(8,128)(2,1)} %w_hbm.1) | copy-start | bytes 3145732
  3.5 91.0 %copy-start.3 = (bf16[256,256]{1,0:T(8,128)(2,1)S(1)}, bf16[256,256]{1,0:T(8,128)(2,1)}, u32[]{:S(2)}) copy-start(bf16[256,256]{1,0:T(8,128)(2,1)} %constant.19.clone.sel_ref) | copy-start | bytes 393220
